TPU v7x, 512 devices: a whole 4x4x16 slice. The times are simulated.
512 devices in a mesh: row: 16 (over x_hi, y, core), col: 32 (over x_lo, z).
Axes of the slice: x: 4 (x_hi: 2, x_lo: 2; x = x_hi * 2 + x_lo), y: 4, z: 16, core: 2. Of those that a mesh axis runs over, the one named last changes fastest.
Arguments:
- positions: float32 [16, 32, 3, 256], P('row', 'col'), may hold values from 0 to 8
- species: int32 [16, 32, 256], P('row', 'col'), may hold values from 0 to 1
- atom_valid: int32 [16, 32, 256], P('row', 'col'), may hold values 0 or 1
- row_count: int32 [16, 32], P('row', 'col'), may hold values from 0 to 1
- col_count: int32 [16, 32], P('row', 'col'), may hold values from 0 to 1
- neighbors: int32 [16, 32, 8, 512], P('row', 'col'), may hold values from 0 to 4607
- basis_rate: float32 [8], replicated, may hold values from 0.005 to 0.1
- radial_weight: bfloat16 [8, 512], replicated, may hold values from -2 to 2
- center_table: bfloat16 [2, 512], replicated, may hold values from -3 to 3
- neighbor_table: bfloat16 [2, 512], replicated, may hold values from -3 to 3
- channel_weight: bfloat16 [512, 64], replicated, may hold values from -0.5 to 0.5
- update_weight: bfloat16 [192, 512], replicated, may hold values from -0.45 to 0.45
- energy_weight: bfloat16 [512], replicated, may hold values from -0.25 to 0.25
Outputs:
- forces: float32 [16, 32, 3, 512], P('row', 'col')
- virial: float32 [16, 32, 9, 512], P('row', 'col')
- energies: float32 [16, 32, 512], P('row', 'col')
Inputs may be any that keep to these rules, and one draw needn't show every extreme that they name: `neighbors`: A neighbour slot naming an empty atom slot is padding.
All inputs are finite; a program needn't handle non-finite values. No bound on the sum of `atom_valid` on one device may be relied on, other than what follows from the above.
Results may differ from a plain program's by a relative error of at most 0.015.
Values sent between devices are 32-bit elements; how exact they have to be, the bound alone decides.
A program may use at most 64 MiB of HBM per device.

v0:
```python
import math

import jax
import jax.numpy as jnp
from jax import lax
from jax.sharding import PartitionSpec as P

K = 8
BA = 128
HAND = 1


SLAB_WIDTH = 8.0
CUT_SQUARE = 64.0
HARM_SCALE = 0.25
ROOT_THREE = math.sqrt(3.0)


def passed_along(value, axis, steps):
    count = lax.axis_size(axis)
    pairs = [(source, (source + steps) % count) for source in range(count)]
    return lax.ppermute(value, axis, pairs)


def padded(cells, sides, width):
    for axis, dim in sides:
        count = lax.axis_size(axis)
        head = lax.slice_in_dim(cells, 0, width, axis=dim)
        tail = lax.slice_in_dim(cells, cells.shape[dim] - width, cells.shape[dim], axis=dim)
        cells = jnp.concatenate(
            [
                lax.ppermute(tail, axis, [(i, (i + 1) % count) for i in range(count)]),
                cells,
                lax.ppermute(head, axis, [((i + 1) % count, i) for i in range(count)]),
            ],
            axis=dim,
        )
    return cells


def atom_energies(
    relative,
    centre_code,
    neighbour_code,
    basis_rate,
    radial_weight,
    center_table,
    neighbor_table,
    channel_weight,
    update_weight,
    energy_weight,
):
    squared = jnp.sum(relative * relative, axis=0)
    active = jnp.logical_and(centre_code[None, :] > 0.5, neighbour_code > 0.5).astype(jnp.float32)
    cutoff = jnp.maximum(1.0 - squared / CUT_SQUARE, 0.0)
    envelope = cutoff * cutoff * active
    radial_basis = (jnp.exp(-basis_rate[:, None, None] * squared[None]) * envelope[None]).astype(
        jnp.bfloat16
    )
    species_ids = jnp.arange(1, center_table.shape[0] + 1).astype(jnp.float32)
    center_hot = (centre_code[None, :] == species_ids[:, None]).astype(jnp.bfloat16)
    neighbour_hot = (neighbour_code[None] == species_ids[:, None, None]).astype(jnp.bfloat16)
    pre_latent = jnp.einsum(
        "rl,rkm->lkm", radial_weight, radial_basis, preferred_element_type=jnp.float32
    )
    pre_latent = (
        pre_latent
        + jnp.einsum("sl,sm->lm", center_table, center_hot, preferred_element_type=jnp.float32)[
            :, None, :
        ]
    )
    pre_latent = pre_latent + jnp.einsum(
        "sl,skm->lkm", neighbor_table, neighbour_hot, preferred_element_type=jnp.float32
    )
    latent = jax.nn.silu(pre_latent)
    latent_low = latent.astype(jnp.bfloat16)
    channel_mix = (
        jnp.einsum("lc,lkm->ckm", channel_weight, latent_low, preferred_element_type=jnp.float32)
        * envelope[None]
    )
    along_x = relative[0] * HARM_SCALE
    along_y = relative[1] * HARM_SCALE
    along_z = relative[2] * HARM_SCALE
    norm_sq = along_x * along_x + along_y * along_y + along_z * along_z
    harmonics = jnp.stack(
        [
            jnp.ones_like(along_x),
            along_x,
            along_y,
            along_z,
            ROOT_THREE * along_x * along_y,
            ROOT_THREE * along_y * along_z,
            0.5 * (3.0 * along_z * along_z - norm_sq),
            ROOT_THREE * along_x * along_z,
            0.5 * ROOT_THREE * (along_x * along_x - along_y * along_y),
        ]
    )
    features = channel_mix[:, None] * harmonics[None]
    density = jnp.sum(features, axis=2) / math.sqrt(relative.shape[1])
    products = features * density[:, :, None]
    scalars = jnp.stack(
        [products[:, 0], jnp.sum(products[:, 1:4], axis=1), jnp.sum(products[:, 4:9], axis=1)]
    )
    channels = scalars.shape[1]
    scalars_low = scalars.reshape((3 * channels,) + scalars.shape[2:]).astype(jnp.bfloat16)
    update = jax.nn.silu(
        jnp.einsum("sl,skm->lkm", update_weight, scalars_low, preferred_element_type=jnp.float32)
    )
    latent_next = (latent + update).astype(jnp.bfloat16)
    edge_energy = (
        jnp.einsum("l,lkm->km", energy_weight, latent_next, preferred_element_type=jnp.float32)
        * envelope
    )
    return jnp.sum(edge_energy, axis=0)


def edge_terms(relative, centre_code, neighbour_code, weights):

    def energy_of(rel_in):
        return atom_energies(rel_in, centre_code, neighbour_code, *weights)

    energy, pullback = jax.vjp(energy_of, relative)
    gradient = pullback(jnp.ones_like(energy))[0]
    return (energy, gradient)


def on_device(
    positions,
    species,
    atom_valid,
    row_count,
    col_count,
    neighbors,
    basis_rate,
    radial_weight,
    center_table,
    neighbor_table,
    channel_weight,
    update_weight,
    energy_weight,
):
    places = positions[0, 0]
    code = (atom_valid[0, 0] * (species[0, 0] + 1)).astype(jnp.float32)
    slots_all = places.shape[1]
    strip = HAND * BA
    strip_block = lax.iota(jnp.int32, strip) // BA
    row_move = (strip_block < row_count[0, 0]).astype(jnp.float32)
    col_move = (strip_block < col_count[0, 0]).astype(jnp.float32)
    middle = jnp.zeros((slots_all - 2 * strip,), jnp.float32)
    leaving = jnp.concatenate([col_move, middle, row_move], axis=0)
    own_kept = jnp.concatenate([places, (code * (1.0 - leaving))[None]], axis=0)
    row_out = jnp.concatenate(
        [places[:, slots_all - strip :], (code[slots_all - strip :] * row_move)[None]], axis=0
    )
    col_out = jnp.concatenate([places[:, :strip], (code[:strip] * col_move)[None]], axis=0)
    row_shift = jnp.array([-SLAB_WIDTH, 0.0, 0.0, 0.0], jnp.float32)[:, None]
    col_shift = jnp.array([0.0, -SLAB_WIDTH, 0.0, 0.0], jnp.float32)[:, None]
    row_in = passed_along(row_out, "row", 1) + row_shift
    col_in = passed_along(col_out, "col", 1) + col_shift
    layout = jnp.concatenate([row_in, col_in, own_kept], axis=1)
    atoms = layout.shape[1]
    beside_all = padded(layout[None, None], (("row", 0), ("col", 1)), 1)
    steps_off = (lax.iota(jnp.float32, 3) - 1.0) * SLAB_WIDTH
    zero_grid = jnp.zeros((3, 3), jnp.float32)
    offset = jnp.stack(
        [
            jnp.broadcast_to(steps_off[:, None], (3, 3)),
            jnp.broadcast_to(steps_off[None, :], (3, 3)),
            zero_grid,
            zero_grid,
        ],
        axis=2,
    )[..., None]
    beside_all = beside_all + offset
    extended = jnp.moveaxis(beside_all, 2, 0).reshape(4, 9 * atoms)
    neighbour_ids = neighbors[0, 0]
    gathered = jnp.take(extended, neighbour_ids, axis=1)
    relative = gathered[:3] - layout[:3][:, None, :]
    neighbour_code = gathered[3]
    blocks = atoms // BA
    rel_blocks = relative.reshape(3, K, blocks, BA).transpose(2, 0, 1, 3)
    centre_blocks = layout[3].reshape(blocks, BA)
    neighbour_blocks = neighbour_code.reshape(K, blocks, BA).transpose(1, 0, 2)
    weights = (
        basis_rate,
        radial_weight,
        center_table,
        neighbor_table,
        channel_weight,
        update_weight,
        energy_weight,
    )

    def block_run(items):
        return edge_terms(items[0], items[1], items[2], weights)

    energy, gradient = lax.map(block_run, (rel_blocks, centre_blocks, neighbour_blocks))
    energy = energy.reshape(atoms)
    gradient = gradient.transpose(1, 2, 0, 3).reshape(3, K, atoms)
    outer = (relative[:, None] * gradient[None]).reshape(9, K, atoms)
    centre_vals = jnp.concatenate(
        [jnp.sum(gradient, axis=1), -0.5 * jnp.sum(outer, axis=1)], axis=0
    )
    ghost_vals = jnp.concatenate([-gradient, -0.5 * outer], axis=0)
    ghost_acc = jnp.zeros((12, 9 * atoms), jnp.float32).at[:, neighbour_ids].add(ghost_vals)
    ghost_grid = ghost_acc.reshape(12, 3, 3, atoms)
    col_part = ghost_grid[:, :, 1]
    for step in (-1, 1):
        col_part = col_part + passed_along(ghost_grid[:, :, 1 + step], "col", step)
    totals = col_part[:, 1]
    for step in (-1, 1):
        totals = totals + passed_along(col_part[:, 1 + step], "row", step)
    final = totals + centre_vals
    return (final[:3][None, None], final[3:][None, None], energy[None, None])


def solution(mesh):
    in_specs = (
        P("row", "col", None, None),
        P("row", "col", None),
        P("row", "col", None),
        P("row", "col"),
        P("row", "col"),
        P("row", "col", None, None),
        P(),
        P(),
        P(),
        P(),
        P(),
        P(),
        P(),
    )
    out_specs = (P("row", "col", None, None), P("row", "col", None, None), P("row", "col", None))
    return jax.shard_map(
        on_device, mesh=mesh, in_specs=in_specs, out_specs=out_specs, check_vma=False
    )
```

profile of v0, /device:TPU:4, one launch (start us, length us, event | category | flops | bytes accessed | tf_op | source)
XLA Modules:
  0.0 189.5 jit_solution(2832817800296338076)
XLA Ops:
  3.3 3.8 %collective-permute-start.1 = (f32[4,128]{1,0:T(4,128)S(1)}, f32[4,128]{1,0:T(4,128)S(1)}, u32[]{:S(2)}, u32[]{:S(2)}) collective-permute-start(f32[4,128]{1,0:T(4,128)S(1)} %pad_maximum_fusion.3), channel_id=1, source_target_pairs={{0,1},{1,2},{2,3},{3,4},{4,5},{5,6},{6,7},{7,8},{8,9},{9,10},{10,1... | collective-permute-start | bytes 6152 | tf_op jit(solution)/shard_map/ppermute | solution.py:22
  7.2 1.9 %collective-permute-start = (f32[4,128]{1,0:T(4,128)S(1)}, f32[4,128]{1,0:T(4,128)S(1)}, u32[]{:S(2)}, u32[]{:S(2)}) collective-permute-start(f32[4,128]{1,0:T(4,128)S(1)} %pad_maximum_fusion.2), channel_id=1, source_target_pairs={{0,32},{32,64},{64,96},{96,128},{128,160},{160,192},{192,224},{224... | collective-permute-start | bytes 6152 | tf_op jit(solution)/shard_map/ppermute | solution.py:22
  10.9 6.0 %collective-permute-done.1 = f32[4,128]{1,0:T(4,128)S(1)} collective-permute-done((f32[4,128]{1,0:T(4,128)S(1)}, f32[4,128]{1,0:T(4,128)S(1)}, u32[]{:S(2)}, u32[]{:S(2)}) %collective-permute-start.1) | collective-permute-done | bytes 2080 | tf_op jit(solution)/shard_map/ppermute | solution.py:22
  18.4 3.7 %collective-permute-start.3 = (f32[1,1,4,512]{3,2,1,0:T(4,128)S(1)}, f32[1,1,4,512]{3,2,1,0:T(4,128)S(1)}, u32[]{:S(2)}, u32[]{:S(2)}) collective-permute-start(f32[1,1,4,512]{3,2,1,0:T(4,128)S(1)} %fusion.127), channel_id=1, source_target_pairs={{32,0},{64,32},{96,64},{128,96},{160,128},{192,160},{224,192},{256... | collective-permute-start | bytes 24584 | tf_op jit(solution)/shard_map/ppermute | solution.py:34
  22.1 1.9 %collective-permute-start.2 = (f32[1,1,4,512]{3,2,1,0:T(4,128)S(1)}, f32[1,1,4,512]{3,2,1,0:T(4,128)S(1)}, u32[]{:S(2)}, u32[]{:S(2)}) collective-permute-start(f32[1,1,4,512]{3,2,1,0:T(4,128)S(1)} %fusion.127), channel_id=1, source_target_pairs={{0,32},{32,64},{64,96},{96,128},{128,160},{160,192},{192,224},{224... | collective-permute-start | bytes 24584 | tf_op jit(solution)/shard_map/ppermute | solution.py:32
  24.7 6.0 %collective-permute-done.2 = f32[1,1,4,512]{3,2,1,0:T(4,128)S(1)} collective-permute-done((f32[1,1,4,512]{3,2,1,0:T(4,128)S(1)}, f32[1,1,4,512]{3,2,1,0:T(4,128)S(1)}, u32[]{:S(2)}, u32[]{:S(2)}) %collective-permute-start.2) | collective-permute-done | bytes 8224 | tf_op jit(solution)/shard_map/ppermute | solution.py:32
  30.7 7.6 %collective-permute-start.5 = (f32[3,1,4,512]{3,2,1,0:T(4,128)S(1)}, f32[3,1,4,512]{3,2,1,0:T(4,128)S(1)}, u32[]{:S(2)}, u32[]{:S(2)}) collective-permute-start(f32[3,1,4,512]{3,2,1,0:T(4,128)S(1)} %pad_maximum_fusion.1), channel_id=1, source_target_pairs={{1,0},{2,1},{3,2},{4,3},{5,4},{6,5},{7,6},{8,7},{9,8},{10,9},{11,1... | collective-permute-start | bytes 73736 | tf_op jit(solution)/shard_map/ppermute | solution.py:34
  38.4 1.9 %collective-permute-start.4 = (f32[3,1,4,512]{3,2,1,0:T(4,128)S(1)}, f32[3,1,4,512]{3,2,1,0:T(4,128)S(1)}, u32[]{:S(2)}, u32[]{:S(2)}) collective-permute-start(f32[3,1,4,512]{3,2,1,0:T(4,128)S(1)} %pad_maximum_fusion.1), channel_id=1, source_target_pairs={{0,1},{1,2},{2,3},{3,4},{4,5},{5,6},{6,7},{7,8},{8,9},{9,10},{10,1... | collective-permute-start | bytes 73736 | tf_op jit(solution)/shard_map/ppermute | solution.py:32
  40.3 5.9 %collective-permute-done.4 = f32[3,1,4,512]{3,2,1,0:T(4,128)S(1)} collective-permute-done((f32[3,1,4,512]{3,2,1,0:T(4,128)S(1)}, f32[3,1,4,512]{3,2,1,0:T(4,128)S(1)}, u32[]{:S(2)}, u32[]{:S(2)}) %collective-permute-start.4) | collective-permute-done | bytes 24608 | tf_op jit(solution)/shard_map/ppermute | solution.py:32
  47.0 14.2 %gather_fusion = f32[4096,4]{1,0:T(8,128)} fusion(f32[4,4608]{0,1:T(8,128)S(1)} %bitcast.479, s32[4096]{0:T(1024)S(1)} %broadcast_clamp_fusion), kind=kCustom, calls=%fused_computation | custom fusion | bytes 147456 | tf_op jit(solution)/shard_map/jit(_take)/gather | solution.py:177
  61.2 2.2 %copy.32 = f32[8,512,4]{1,0,2:T(8,128)S(1)} copy(f32[8,512,4]{2,1,0:T(8,128)} %bitcast.480) | data formatting | bytes 131072 | tf_op jit(solution)/shard_map/jit(_take)/gather | solution.py:177
  64.7 71.5 %while.15 = (s32[]{:T(128)}, f32[4,128]{1,0:T(4,128)}, f32[4,3,8,128]{3,2,0,1:T(8,128)}, f32[8,1,1]{0,2,1:T(1,128)S(1)}, f32[4,3,8,128]{3,2,0,1:T(8,128)}, /*ind...) while((s32[]{:T(128)}, f32[4,128]{1,0:T(4,128)}, ...), condition=%wide.region_12.13_spmd, body=%wide.region_0.12_spmd.sunk | while | flops 591755008 | bytes 43942624 | solution.py:197
  69.2 1.4 broadcast_multiply_fusion.7
  71.4 1.4 fusion.171
  74.1 2.0 %fusion.173 = f32[192,8,128]{2,0,1:T(8,128)S(1)} fusion(f32[8,128,512]{2,1,0:T(8,128)S(1)} %fusion.171, f32[512]{0:T(512)S(1)} %convert.48, f32[8,128]{1,0:T(8,128)S(1)} %get-tuple-element.375, bf16[192,512]{1,0:T(8,128)(2,1)} %get-tuple-element.428), kind=kOutput, calls=%fused_computation.41.clone.1 | convolution fusion | flops 208011264 | bytes 3086336 | tf_op jit(solution)/shard_map/while/body/eval_jaxpr/transpose(jvp(sl,skm->lkm))/dot_general | solution.py:107
  76.1 1.3 dynamic_update_slice.20
  79.0 2.1 %multiply_reduce_fusion.16 = (f32[8,128]{1,0:T(8,128)S(1)}, f32[8,128]{1,0:T(8,128)S(1)}) fusion(f32[8,128]{1,0:T(8,128)S(1)} %fusion.167, f32[8]{0:T(128)} %bitcast.499, f32[8,128]{1,0:T(8,128)S(1)} %get-tuple-element.371, bf16[8,512]{1,0:T(8,128)(2,1)S(1)} %get-tuple-element.424, f32[512,8,128]{0,2,1:T(8,128)S(1)} %bitcast_add_fusion.6, ...), kind=kOutput, calls=%fused_computation.73.clone.1 | convolution fusion | flops 83499008 | bytes 2455584 | tf_op jit(solution)/shard_map/while/body/eval_jaxpr/transpose(jvp(rl,rkm->lkm))/dot_general | solution.py:63
  81.2 1.3 fusion.179
  87.0 1.4 broadcast_multiply_fusion.7
  89.3 1.4 fusion.171
  92.0 2.0 %fusion.173 = f32[192,8,128]{2,0,1:T(8,128)S(1)} fusion(f32[8,128,512]{2,1,0:T(8,128)S(1)} %fusion.171, f32[512]{0:T(512)S(1)} %convert.48, f32[8,128]{1,0:T(8,128)S(1)} %get-tuple-element.375, bf16[192,512]{1,0:T(8,128)(2,1)} %get-tuple-element.428), kind=kOutput, calls=%fused_computation.41.clone.1 | convolution fusion | flops 208011264 | bytes 3086336 | tf_op jit(solution)/shard_map/while/body/eval_jaxpr/transpose(jvp(sl,skm->lkm))/dot_general | solution.py:107
  94.0 1.3 dynamic_update_slice.20
  96.8 2.1 %multiply_reduce_fusion.16 = (f32[8,128]{1,0:T(8,128)S(1)}, f32[8,128]{1,0:T(8,128)S(1)}) fusion(f32[8,128]{1,0:T(8,128)S(1)} %fusion.167, f32[8]{0:T(128)} %bitcast.499, f32[8,128]{1,0:T(8,128)S(1)} %get-tuple-element.371, bf16[8,512]{1,0:T(8,128)(2,1)S(1)} %get-tuple-element.424, f32[512,8,128]{0,2,1:T(8,128)S(1)} %bitcast_add_fusion.6, ...), kind=kOutput, calls=%fused_computation.73.clone.1 | convolution fusion | flops 83499008 | bytes 2455584 | tf_op jit(solution)/shard_map/while/body/eval_jaxpr/transpose(jvp(rl,rkm->lkm))/dot_general | solution.py:63
  99.1 1.3 fusion.179
  104.9 1.4 broadcast_multiply_fusion.7
  107.1 1.4 fusion.171
  109.8 2.0 %fusion.173 = f32[192,8,128]{2,0,1:T(8,128)S(1)} fusion(f32[8,128,512]{2,1,0:T(8,128)S(1)} %fusion.171, f32[512]{0:T(512)S(1)} %convert.48, f32[8,128]{1,0:T(8,128)S(1)} %get-tuple-element.375, bf16[192,512]{1,0:T(8,128)(2,1)} %get-tuple-element.428), kind=kOutput, calls=%fused_computation.41.clone.1 | convolution fusion | flops 208011264 | bytes 3086336 | tf_op jit(solution)/shard_map/while/body/eval_jaxpr/transpose(jvp(sl,skm->lkm))/dot_general | solution.py:107
  111.9 1.3 dynamic_update_slice.20
  114.7 2.1 %multiply_reduce_fusion.16 = (f32[8,128]{1,0:T(8,128)S(1)}, f32[8,128]{1,0:T(8,128)S(1)}) fusion(f32[8,128]{1,0:T(8,128)S(1)} %fusion.167, f32[8]{0:T(128)} %bitcast.499, f32[8,128]{1,0:T(8,128)S(1)} %get-tuple-element.371, bf16[8,512]{1,0:T(8,128)(2,1)S(1)} %get-tuple-element.424, f32[512,8,128]{0,2,1:T(8,128)S(1)} %bitcast_add_fusion.6, ...), kind=kOutput, calls=%fused_computation.73.clone.1 | convolution fusion | flops 83499008 | bytes 2455584 | tf_op jit(solution)/shard_map/while/body/eval_jaxpr/transpose(jvp(rl,rkm->lkm))/dot_general | solution.py:63
  116.9 1.3 fusion.179
  121.5 1.2 bitcast_add_fusion.6
  122.8 1.4 broadcast_multiply_fusion.7
  125.0 1.4 fusion.171
  127.7 2.0 %fusion.173 = f32[192,8,128]{2,0,1:T(8,128)S(1)} fusion(f32[8,128,512]{2,1,0:T(8,128)S(1)} %fusion.171, f32[512]{0:T(512)S(1)} %convert.48, f32[8,128]{1,0:T(8,128)S(1)} %get-tuple-element.375, bf16[192,512]{1,0:T(8,128)(2,1)} %get-tuple-element.428), kind=kOutput, calls=%fused_computation.41.clone.1 | convolution fusion | flops 208011264 | bytes 3086336 | tf_op jit(solution)/shard_map/while/body/eval_jaxpr/transpose(jvp(sl,skm->lkm))/dot_general | solution.py:107
  129.7 1.3 dynamic_update_slice.20
  132.6 2.1 %multiply_reduce_fusion.16 = (f32[8,128]{1,0:T(8,128)S(1)}, f32[8,128]{1,0:T(8,128)S(1)}) fusion(f32[8,128]{1,0:T(8,128)S(1)} %fusion.167, f32[8]{0:T(128)} %bitcast.499, f32[8,128]{1,0:T(8,128)S(1)} %get-tuple-element.371, bf16[8,512]{1,0:T(8,128)(2,1)S(1)} %get-tuple-element.424, f32[512,8,128]{0,2,1:T(8,128)S(1)} %bitcast_add_fusion.6, ...), kind=kOutput, calls=%fused_computation.73.clone.1 | convolution fusion | flops 83499008 | bytes 2455584 | tf_op jit(solution)/shard_map/while/body/eval_jaxpr/transpose(jvp(rl,rkm->lkm))/dot_general | solution.py:63
  134.8 1.3 fusion.179
  137.9 2.0 %copy.43 = f32[8,512,12]{2,1,0:T(8,128)} copy(f32[8,512,12]{1,0,2:T(8,128)S(1)} %maximum_bitcast_fusion) | data formatting | bytes 393216 | tf_op jit(solution)/shard_map/concatenate | solution.py:204
  139.9 23.2 %scatter_custom_fusion = f32[12,4608]{0,1:T(8,128)S(1)} fusion(s32[4096]{0:T(1024)} %bitcast.494, f32[4096,12]{1,0:T(8,128)} %bitcast.481, f32[]{:T(128)} %constant.152.clone.1), kind=kCustom, calls=%fused_computation.178 | custom fusion | flops 49152 | bytes 221696 | tf_op jit(solution)/shard_map/scatter-add | solution.py:205
  163.1 1.3 fusion.121
  164.4 1.4 copy.49
  165.8 1.4 copy.50
  167.2 1.9 %collective-permute-start.7 = (f32[12,3,512]{2,0,1:T(8,128)S(1)}, f32[12,3,512]{2,0,1:T(8,128)S(1)}, u32[]{:S(2)}, u32[]{:S(2)}) collective-permute-start(f32[12,3,512]{2,0,1:T(8,128)S(1)} %bitcast.487), channel_id=1, source_target_pairs={{0,1},{1,2},{2,3},{3,4},{4,5},{5,6},{6,7},{7,8},{8,9},{9,10},{10,1... | collective-permute-start | bytes 221192 | tf_op jit(solution)/shard_map/ppermute | solution.py:22
  169.2 6.0 %collective-permute-start.6 = (f32[12,3,512]{2,0,1:T(8,128)S(1)}, f32[12,3,512]{2,0,1:T(8,128)S(1)}, u32[]{:S(2)}, u32[]{:S(2)}) collective-permute-start(f32[12,3,512]{2,0,1:T(8,128)S(1)} %bitcast.486), channel_id=1, source_target_pairs={{0,31},{1,0},{2,1},{3,2},{4,3},{5,4},{6,5},{7,6},{8,7},{9,8},{10,9... | collective-permute-start | bytes 221192 | tf_op jit(solution)/shard_map/ppermute | solution.py:22
  175.8 1.5 collective-permute-done.6
  177.4 1.9 %collective-permute-start.8 = (f32[12,512]{1,0:T(8,128)S(1)}, f32[12,512]{1,0:T(8,128)S(1)}, u32[]{:S(2)}, u32[]{:S(2)}) collective-permute-start(f32[12,512]{1,0:T(8,128)S(1)} %get-tuple-element.268), channel_id=1, source_target_pairs={{0,480},{32,0},{64,32},{96,64},{128,96},{160,128},{192,160},{224,1... | collective-permute-start | bytes 73736 | tf_op jit(solution)/shard_map/ppermute | solution.py:22
  179.4 2.4 %collective-permute-start.9 = (f32[12,512]{1,0:T(8,128)S(1)}, f32[12,512]{1,0:T(8,128)S(1)}, u32[]{:S(2)}, u32[]{:S(2)}) collective-permute-start(f32[12,512]{1,0:T(8,128)S(1)} %get-tuple-element.269), channel_id=1, source_target_pairs={{0,32},{32,64},{64,96},{96,128},{128,160},{160,192},{192,224},{224... | collective-permute-start | bytes 73736 | tf_op jit(solution)/shard_map/ppermute | solution.py:22
  181.8 6.4 %collective-permute-done.9 = f32[12,512]{1,0:T(8,128)S(1)} collective-permute-done((f32[12,512]{1,0:T(8,128)S(1)}, f32[12,512]{1,0:T(8,128)S(1)}, u32[]{:S(2)}, u32[]{:S(2)}) %collective-permute-start.9) | collective-permute-done | bytes 24608 | tf_op jit(solution)/shard_map/ppermute | solution.py:22
  (317 shorter events, 41.5 us)
Async XLA Ops:
  3.3 13.6 %collective-permute-start.1 = (f32[4,128]{1,0:T(4,128)S(1)}, f32[4,128]{1,0:T(4,128)S(1)}, u32[]{:S(2)}, u32[]{:S(2)}) collective-permute-start(f32[4,128]{1,0:T(4,128)S(1)} %pad_maximum_fusion.3), channel_id=1, source_target_pairs={{0,1},{1,2},{2,3},{3,4},{4,5},{5,6},{6,7},{7,8},{8,9},{9,10},{10,1... | collective-permute-start | bytes 6152 | tf_op jit(solution)/shard_map/ppermute | solution.py:22
  7.2 10.5 %collective-permute-start = (f32[4,128]{1,0:T(4,128)S(1)}, f32[4,128]{1,0:T(4,128)S(1)}, u32[]{:S(2)}, u32[]{:S(2)}) collective-permute-start(f32[4,128]{1,0:T(4,128)S(1)} %pad_maximum_fusion.2), channel_id=1, source_target_pairs={{0,32},{32,64},{64,96},{96,128},{128,160},{160,192},{192,224},{224... | collective-permute-start | bytes 6152 | tf_op jit(solution)/shard_map/ppermute | solution.py:22
  10.6 35.6 %copy-start.8 = (s32[1,4,8,128]{3,1,2,0:T(4,128)}, s32[1,4,8,128]{3,1,2,0:T(4,128)S(1)}, u32[]{:S(2)}) copy-start(s32[1,4,8,128]{3,1,2,0:T(4,128)S(1)} %copy.53) | copy-start | bytes 49156
  18.4 6.3 %collective-permute-start.3 = (f32[1,1,4,512]{3,2,1,0:T(4,128)S(1)}, f32[1,1,4,512]{3,2,1,0:T(4,128)S(1)}, u32[]{:S(2)}, u32[]{:S(2)}) collective-permute-start(f32[1,1,4,512]{3,2,1,0:T(4,128)S(1)} %fusion.127), channel_id=1, source_target_pairs={{32,0},{64,32},{96,64},{128,96},{160,128},{192,160},{224,192},{256... | collective-permute-start | bytes 24584 | tf_op jit(solution)/shard_map/ppermute | solution.py:34
  22.1 8.6 %collective-permute-start.2 = (f32[1,1,4,512]{3,2,1,0:T(4,128)S(1)}, f32[1,1,4,512]{3,2,1,0:T(4,128)S(1)}, u32[]{:S(2)}, u32[]{:S(2)}) collective-permute-start(f32[1,1,4,512]{3,2,1,0:T(4,128)S(1)} %fusion.127), channel_id=1, source_target_pairs={{0,32},{32,64},{64,96},{96,128},{128,160},{160,192},{192,224},{224... | collective-permute-start | bytes 24584 | tf_op jit(solution)/shard_map/ppermute | solution.py:32
  30.7 9.6 %collective-permute-start.5 = (f32[3,1,4,512]{3,2,1,0:T(4,128)S(1)}, f32[3,1,4,512]{3,2,1,0:T(4,128)S(1)}, u32[]{:S(2)}, u32[]{:S(2)}) collective-permute-start(f32[3,1,4,512]{3,2,1,0:T(4,128)S(1)} %pad_maximum_fusion.1), channel_id=1, source_target_pairs={{1,0},{2,1},{3,2},{4,3},{5,4},{6,5},{7,6},{8,7},{9,8},{10,9},{11,1... | collective-permute-start | bytes 73736 | tf_op jit(solution)/shard_map/ppermute | solution.py:34
  38.4 7.8 %collective-permute-start.4 = (f32[3,1,4,512]{3,2,1,0:T(4,128)S(1)}, f32[3,1,4,512]{3,2,1,0:T(4,128)S(1)}, u32[]{:S(2)}, u32[]{:S(2)}) collective-permute-start(f32[3,1,4,512]{3,2,1,0:T(4,128)S(1)} %pad_maximum_fusion.1), channel_id=1, source_target_pairs={{0,1},{1,2},{2,3},{3,4},{4,5},{5,6},{6,7},{7,8},{8,9},{9,10},{10,1... | collective-permute-start | bytes 73736 | tf_op jit(solution)/shard_map/ppermute | solution.py:32
  47.0 17.7 %copy-start.2 = (bf16[8,512]{1,0:T(8,128)(2,1)S(1)}, bf16[8,512]{1,0:T(8,128)(2,1)}, u32[]{:S(2)}) copy-start(bf16[8,512]{1,0:T(8,128)(2,1)} %param.24) | copy-start | bytes 24580
  47.0 17.7 %copy-start.3 = (bf16[512]{0:T(512)(128)(2,1)S(1)}, bf16[512]{0:T(512)(128)(2,1)}, u32[]{:S(2)}) copy-start(bf16[512]{0:T(512)(128)(2,1)} %param.29) | copy-start | bytes 3076
  47.0 17.7 %copy-start.15 = (bf16[512,64]{0,1:T(8,128)(2,1)S(1)}, bf16[512,64]{0,1:T(8,128)(2,1)}, u32[]{:S(2)}) copy-start(bf16[512,64]{0,1:T(8,128)(2,1)} %param.27) | copy-start | bytes 196612
  64.7 4.5 %copy-start.6 = (f32[4,8,128]{2,1,0:T(8,128)}, f32[4,8,128]{2,1,0:T(8,128)S(1)}, u32[]{:S(2)}) copy-start(f32[4,8,128]{2,1,0:T(8,128)S(1)} %get-tuple-element.423) | copy-start | bytes 49156 | tf_op jit(solution)/shard_map/while
  64.7 4.5 %copy-start.11 = (f32[8,1,1]{0,2,1:T(1,128)}, f32[8,1,1]{0,2,1:T(1,128)S(1)}, u32[]{:S(2)}) copy-start(f32[8,1,1]{0,2,1:T(1,128)S(1)} %get-tuple-element.420) | copy-start | bytes 100 | tf_op jit(solution)/shard_map/while
  64.7 4.5 %copy-start.13 = (f32[4,128]{1,0:T(4,128)}, f32[4,128]{1,0:T(4,128)S(1)}, u32[]{:S(2)}) copy-start(f32[4,128]{1,0:T(4,128)S(1)} %get-tuple-element.422) | copy-start | bytes 6148 | tf_op jit(solution)/shard_map/while
  64.8 9.3 %copy-start.9 = (f32[512]{0:T(512)}, f32[512]{0:T(512)S(1)}, u32[]{:S(2)}) copy-start(f32[512]{0:T(512)S(1)} %convert.48) | copy-start | bytes 6148 | tf_op jit(solution)/shard_map/while
  78.9 2.2 %copy-start = (f32[64,8,128]{2,0,1:T(8,128)S(1)}, f32[64,8,128]{2,0,1:T(8,128)}, u32[]{:S(2)}) copy-start(f32[64,8,128]{2,0,1:T(8,128)} %get-tuple-element.386) | copy-start | bytes 786436 | tf_op jit(solution)/shard_map/while
  78.9 3.6 %copy-start.7 = (f32[4,8,128]{2,1,0:T(8,128)S(1)}, f32[4,8,128]{2,1,0:T(8,128)}, u32[]{:S(2)}) copy-start(f32[4,8,128]{2,1,0:T(8,128)} %copy-done.6) | copy-start | bytes 49156 | tf_op jit(solution)/shard_map/while
  78.9 3.6 %copy-start.12 = (f32[8,1,1]{0,2,1:T(1,128)S(1)}, f32[8,1,1]{0,2,1:T(1,128)}, u32[]{:S(2)}) copy-start(f32[8,1,1]{0,2,1:T(1,128)} %copy-done.11) | copy-start | bytes 100 | tf_op jit(solution)/shard_map/while
  79.0 3.6 %copy-start.14 = (f32[4,128]{1,0:T(4,128)S(1)}, f32[4,128]{1,0:T(4,128)}, u32[]{:S(2)}) copy-start(f32[4,128]{1,0:T(4,128)} %copy-done.13) | copy-start | bytes 6148 | tf_op jit(solution)/shard_map/while
  79.0 3.6 %copy-start.16 = (bf16[512,64]{0,1:T(8,128)(2,1)S(1)}, bf16[512,64]{0,1:T(8,128)(2,1)}, u32[]{:S(2)}) copy-start(bf16[512,64]{0,1:T(8,128)(2,1)} %get-tuple-element.467) | copy-start | bytes 196612 | tf_op jit(solution)/shard_map/while
  82.6 4.4 %copy-start.6 = (f32[4,8,128]{2,1,0:T(8,128)}, f32[4,8,128]{2,1,0:T(8,128)S(1)}, u32[]{:S(2)}) copy-start(f32[4,8,128]{2,1,0:T(8,128)S(1)} %get-tuple-element.423) | copy-start | bytes 49156 | tf_op jit(solution)/shard_map/while
  82.6 4.4 %copy-start.11 = (f32[8,1,1]{0,2,1:T(1,128)}, f32[8,1,1]{0,2,1:T(1,128)S(1)}, u32[]{:S(2)}) copy-start(f32[8,1,1]{0,2,1:T(1,128)S(1)} %get-tuple-element.420) | copy-start | bytes 100 | tf_op jit(solution)/shard_map/while
  82.6 4.4 %copy-start.13 = (f32[4,128]{1,0:T(4,128)}, f32[4,128]{1,0:T(4,128)S(1)}, u32[]{:S(2)}) copy-start(f32[4,128]{1,0:T(4,128)S(1)} %get-tuple-element.422) | copy-start | bytes 6148 | tf_op jit(solution)/shard_map/while
  82.7 9.3 %copy-start.9 = (f32[512]{0:T(512)}, f32[512]{0:T(512)S(1)}, u32[]{:S(2)}) copy-start(f32[512]{0:T(512)S(1)} %convert.48) | copy-start | bytes 6148 | tf_op jit(solution)/shard_map/while
  96.8 3.6 %copy-start.7 = (f32[4,8,128]{2,1,0:T(8,128)S(1)}, f32[4,8,128]{2,1,0:T(8,128)}, u32[]{:S(2)}) copy-start(f32[4,8,128]{2,1,0:T(8,128)} %copy-done.6) | copy-start | bytes 49156 | tf_op jit(solution)/shard_map/while
  96.8 3.6 %copy-start.12 = (f32[8,1,1]{0,2,1:T(1,128)S(1)}, f32[8,1,1]{0,2,1:T(1,128)}, u32[]{:S(2)}) copy-start(f32[8,1,1]{0,2,1:T(1,128)} %copy-done.11) | copy-start | bytes 100 | tf_op jit(solution)/shard_map/while
  96.8 3.6 %copy-start.14 = (f32[4,128]{1,0:T(4,128)S(1)}, f32[4,128]{1,0:T(4,128)}, u32[]{:S(2)}) copy-start(f32[4,128]{1,0:T(4,128)} %copy-done.13) | copy-start | bytes 6148 | tf_op jit(solution)/shard_map/while
  96.8 3.6 %copy-start.16 = (bf16[512,64]{0,1:T(8,128)(2,1)S(1)}, bf16[512,64]{0,1:T(8,128)(2,1)}, u32[]{:S(2)}) copy-start(bf16[512,64]{0,1:T(8,128)(2,1)} %get-tuple-element.467) | copy-start | bytes 196612 | tf_op jit(solution)/shard_map/while
  100.4 4.4 %copy-start.6 = (f32[4,8,128]{2,1,0:T(8,128)}, f32[4,8,128]{2,1,0:T(8,128)S(1)}, u32[]{:S(2)}) copy-start(f32[4,8,128]{2,1,0:T(8,128)S(1)} %get-tuple-element.423) | copy-start | bytes 49156 | tf_op jit(solution)/shard_map/while
  100.4 4.4 %copy-start.11 = (f32[8,1,1]{0,2,1:T(1,128)}, f32[8,1,1]{0,2,1:T(1,128)S(1)}, u32[]{:S(2)}) copy-start(f32[8,1,1]{0,2,1:T(1,128)S(1)} %get-tuple-element.420) | copy-start | bytes 100 | tf_op jit(solution)/shard_map/while
  100.4 4.4 %copy-start.13 = (f32[4,128]{1,0:T(4,128)}, f32[4,128]{1,0:T(4,128)S(1)}, u32[]{:S(2)}) copy-start(f32[4,128]{1,0:T(4,128)S(1)} %get-tuple-element.422) | copy-start | bytes 6148 | tf_op jit(solution)/shard_map/while
  100.5 9.3 %copy-start.9 = (f32[512]{0:T(512)}, f32[512]{0:T(512)S(1)}, u32[]{:S(2)}) copy-start(f32[512]{0:T(512)S(1)} %convert.48) | copy-start | bytes 6148 | tf_op jit(solution)/shard_map/while
  114.6 3.6 %copy-start.7 = (f32[4,8,128]{2,1,0:T(8,128)S(1)}, f32[4,8,128]{2,1,0:T(8,128)}, u32[]{:S(2)}) copy-start(f32[4,8,128]{2,1,0:T(8,128)} %copy-done.6) | copy-start | bytes 49156 | tf_op jit(solution)/shard_map/while
  114.7 3.6 %copy-start.12 = (f32[8,1,1]{0,2,1:T(1,128)S(1)}, f32[8,1,1]{0,2,1:T(1,128)}, u32[]{:S(2)}) copy-start(f32[8,1,1]{0,2,1:T(1,128)} %copy-done.11) | copy-start | bytes 100 | tf_op jit(solution)/shard_map/while
  114.7 3.6 %copy-start.14 = (f32[4,128]{1,0:T(4,128)S(1)}, f32[4,128]{1,0:T(4,128)}, u32[]{:S(2)}) copy-start(f32[4,128]{1,0:T(4,128)} %copy-done.13) | copy-start | bytes 6148 | tf_op jit(solution)/shard_map/while
  114.7 3.6 %copy-start.16 = (bf16[512,64]{0,1:T(8,128)(2,1)S(1)}, bf16[512,64]{0,1:T(8,128)(2,1)}, u32[]{:S(2)}) copy-start(bf16[512,64]{0,1:T(8,128)(2,1)} %get-tuple-element.467) | copy-start | bytes 196612 | tf_op jit(solution)/shard_map/while
  118.3 4.5 %copy-start.6 = (f32[4,8,128]{2,1,0:T(8,128)}, f32[4,8,128]{2,1,0:T(8,128)S(1)}, u32[]{:S(2)}) copy-start(f32[4,8,128]{2,1,0:T(8,128)S(1)} %get-tuple-element.423) | copy-start | bytes 49156 | tf_op jit(solution)/shard_map/while
  118.3 4.5 %copy-start.11 = (f32[8,1,1]{0,2,1:T(1,128)}, f32[8,1,1]{0,2,1:T(1,128)S(1)}, u32[]{:S(2)}) copy-start(f32[8,1,1]{0,2,1:T(1,128)S(1)} %get-tuple-element.420) | copy-start | bytes 100 | tf_op jit(solution)/shard_map/while
  118.3 4.5 %copy-start.13 = (f32[4,128]{1,0:T(4,128)}, f32[4,128]{1,0:T(4,128)S(1)}, u32[]{:S(2)}) copy-start(f32[4,128]{1,0:T(4,128)S(1)} %get-tuple-element.422) | copy-start | bytes 6148 | tf_op jit(solution)/shard_map/while
  118.4 9.3 %copy-start.9 = (f32[512]{0:T(512)}, f32[512]{0:T(512)S(1)}, u32[]{:S(2)}) copy-start(f32[512]{0:T(512)S(1)} %convert.48) | copy-start | bytes 6148 | tf_op jit(solution)/shard_map/while
  132.5 3.6 %copy-start.7 = (f32[4,8,128]{2,1,0:T(8,128)S(1)}, f32[4,8,128]{2,1,0:T(8,128)}, u32[]{:S(2)}) copy-start(f32[4,8,128]{2,1,0:T(8,128)} %copy-done.6) | copy-start | bytes 49156 | tf_op jit(solution)/shard_map/while
  132.5 3.6 %copy-start.12 = (f32[8,1,1]{0,2,1:T(1,128)S(1)}, f32[8,1,1]{0,2,1:T(1,128)}, u32[]{:S(2)}) copy-start(f32[8,1,1]{0,2,1:T(1,128)} %copy-done.11) | copy-start | bytes 100 | tf_op jit(solution)/shard_map/while
  132.5 3.6 %copy-start.14 = (f32[4,128]{1,0:T(4,128)S(1)}, f32[4,128]{1,0:T(4,128)}, u32[]{:S(2)}) copy-start(f32[4,128]{1,0:T(4,128)} %copy-done.13) | copy-start | bytes 6148 | tf_op jit(solution)/shard_map/while
  132.6 3.6 %copy-start.16 = (bf16[512,64]{0,1:T(8,128)(2,1)S(1)}, bf16[512,64]{0,1:T(8,128)(2,1)}, u32[]{:S(2)}) copy-start(bf16[512,64]{0,1:T(8,128)(2,1)} %get-tuple-element.467) | copy-start | bytes 196612 | tf_op jit(solution)/shard_map/while
  164.4 17.4 %copy-start.1 = (f32[4,3,8,128]{3,2,0,1:T(8,128)S(1)}, f32[4,3,8,128]{3,2,0,1:T(8,128)}, u32[]{:S(2)}) copy-start(f32[4,3,8,128]{3,2,0,1:T(8,128)} %get-tuple-element.454) | copy-start | bytes 147460
  167.2 8.6 %collective-permute-start.7 = (f32[12,3,512]{2,0,1:T(8,128)S(1)}, f32[12,3,512]{2,0,1:T(8,128)S(1)}, u32[]{:S(2)}, u32[]{:S(2)}) collective-permute-start(f32[12,3,512]{2,0,1:T(8,128)S(1)} %bitcast.487), channel_id=1, source_target_pairs={{0,1},{1,2},{2,3},{3,4},{4,5},{5,6},{6,7},{7,8},{8,9},{9,10},{10,1... | collective-permute-start | bytes 221192 | tf_op jit(solution)/shard_map/ppermute | solution.py:22
  169.2 8.2 %collective-permute-start.6 = (f32[12,3,512]{2,0,1:T(8,128)S(1)}, f32[12,3,512]{2,0,1:T(8,128)S(1)}, u32[]{:S(2)}, u32[]{:S(2)}) collective-permute-start(f32[12,3,512]{2,0,1:T(8,128)S(1)} %bitcast.486), channel_id=1, source_target_pairs={{0,31},{1,0},{2,1},{3,2},{4,3},{5,4},{6,5},{7,6},{8,7},{9,8},{10,9... | collective-permute-start | bytes 221192 | tf_op jit(solution)/shard_map/ppermute | solution.py:22
  177.4 4.4 %collective-permute-start.8 = (f32[12,512]{1,0:T(8,128)S(1)}, f32[12,512]{1,0:T(8,128)S(1)}, u32[]{:S(2)}, u32[]{:S(2)}) collective-permute-start(f32[12,512]{1,0:T(8,128)S(1)} %get-tuple-element.268), channel_id=1, source_target_pairs={{0,480},{32,0},{64,32},{96,64},{128,96},{160,128},{192,160},{224,1... | collective-permute-start | bytes 73736 | tf_op jit(solution)/shard_map/ppermute | solution.py:22
  179.4 8.8 %collective-permute-start.9 = (f32[12,512]{1,0:T(8,128)S(1)}, f32[12,512]{1,0:T(8,128)S(1)}, u32[]{:S(2)}, u32[]{:S(2)}) collective-permute-start(f32[12,512]{1,0:T(8,128)S(1)} %get-tuple-element.269), channel_id=1, source_target_pairs={{0,32},{32,64},{64,96},{96,128},{128,160},{160,192},{192,224},{224... | collective-permute-start | bytes 73736 | tf_op jit(solution)/shard_map/ppermute | solution.py:22
  (15 other events, 21.1 us)
where the time goes:
time: 191 us; the launch traced here: 189 us
  other arithmetic  47.3 us (25%)
  matrix products  43.6 us (23%)
  local copies, waits for them, and re-layouts  35.3 us (18%)
  starting transfers between devices  33.2 us (17%)
  waiting for transfers between devices  26.2 us (14%)
  between operations  2.23 us (1%)
    scatter-add x1, other arithmetic, on_device(): jnp.zeros((12, 9 * atoms), jnp.float32).at[:, neighbour_ids].add(ghost_vals)  23.2 us
    ppermute x6, starting transfers between devices, passed_along(): return lax.ppermute(value, axis, pairs)  18 us
    gather x2, local copies, waits for them, and re-layouts, on_device(): gathered = jnp.take(extended, neighbour_ids, axis=1)  16.4 us
    ppermute x6, waiting for transfers between devices, passed_along(): return lax.ppermute(value, axis, pairs)  14.3 us
    dot_general x8, matrix products, atom_energies(): jnp.einsum('sl,skm->lkm', update_weight, scalars_low, preferred_element_t...  13.5 us
    ppermute x2, waiting for transfers between devices, padded(): lax.ppermute(tail, axis, [(i, (i + 1) % count) for i in range(count)])  11.9 us
    ppermute x2, starting transfers between devices, padded(): lax.ppermute(head, axis, [((i + 1) % count, i) for i in range(count)])  11.4 us
    dot_general x8, matrix products, atom_energies(): jnp.einsum('rl,rkm->lkm', radial_weight, radial_basis, preferred_element_...  10.7 us
  transfers between devices with their start and end apart: 10, of which 6 were waited for; matrix products, arithmetic and copies ran while one was open for 2% of the time, Pallas kernels for 0%

commit v1 on v0

v1 whole, which is shorter than its diff:
```python
import functools
import math

import jax
import jax.numpy as jnp
from jax import lax
from jax.experimental import pallas as pl
from jax.experimental.pallas import tpu as pltpu
from jax.sharding import PartitionSpec as P

K = 8
BA = 128
C = 64
LAT = 512
ATOMS = 512
SPAN = 256
GROUPS = 18
SLAB = 8.0
SCALE = 0.25
ROOT3 = math.sqrt(3.0)
NORM = 1.0 / math.sqrt(8.0)
F32 = jnp.float32
BF16 = jnp.bfloat16
MESH = pl.DeviceIdType.MESH

NEAR = [(a, b) for a in (-1, 0, 1) for b in (-1, 0, 1) if (a, b) != (0, 0)]
REACH = NEAR + [(2, b) for b in (-1, 0, 1)] + [(a, 2) for a in (-1, 0, 1)]
DEGREE = [0, 1, 1, 1, 2, 2, 2, 2, 2]
CHUNK = 128


def dot(a, b):
    return lax.dot_general(a, b, (((1,), (0,)), ((), ())), preferred_element_type=F32)


def dot_nt(a, b):
    return lax.dot_general(a, b, (((1,), (1,)), ((), ())), preferred_element_type=F32)


def kernel(
    n_row,
    n_col,
    pos,
    spc,
    valid,
    rcount,
    ccount,
    nbr,
    rate,
    rw,
    ct,
    nt,
    cw,
    uw,
    ew,
    forces,
    virial,
    energies,
    own,
    inbox,
    near_table,
    rel_code,
    onehot,
    harm,
    edge,
    w_stage,
    w1t,
    w1,
    wut,
    wue,
    wct,
    wcc,
    ew16,
    latent,
    slope1,
    updated,
    slope2,
    mix0,
    mix,
    dens,
    ddens,
    prods,
    scal,
    dscal,
    dmix,
    dharm,
    dlow,
    dpre,
    vals,
    ghost,
    ghost_in,
    send_in,
    recv_in,
    send_out,
    recv_out,
):
    row = lax.axis_index("row")
    col = lax.axis_index("col")

    def at(dr, dc):
        return (lax.rem(row + (dr + n_row), n_row), lax.rem(col + (dc + n_col), n_col))

    barrier = pltpu.get_barrier_semaphore()
    for dr, dc in REACH:
        pl.semaphore_signal(barrier, inc=1, device_id=at(-dr, -dc), device_id_type=MESH)

    code = (valid[0] * (spc[0] + 1)).astype(F32)
    moves = jnp.concatenate(
        [
            jnp.where(jnp.broadcast_to(ccount[...], (1, BA)) > 0, 1.0, 0.0),
            jnp.where(jnp.broadcast_to(rcount[...], (1, BA)) > 0, 1.0, 0.0),
        ],
        axis=1,
    )
    own[...] = jnp.zeros_like(own)
    own[0:3, :] = pos[0, 0]
    own[3:4, :] = code * (1.0 - moves)
    own[4:5, :] = code * moves
    pl.semaphore_wait(barrier, len(REACH))
    sends = []
    for slot, (dr, dc) in enumerate(REACH):
        copy = pltpu.make_async_remote_copy(
            src_ref=own,
            dst_ref=inbox.at[slot],
            send_sem=send_in.at[slot],
            recv_sem=recv_in.at[slot],
            device_id=at(dr, dc),
            device_id_type=MESH,
        )
        copy.start()
        sends.append(copy)

    w_stage[...] = jnp.zeros_like(w_stage)
    w_stage[0:8, :] = rw[...].astype(F32) * 0.5
    w_stage[8:10, :] = ct[...].astype(F32) * 0.5
    w_stage[10:12, :] = nt[...].astype(F32) * 0.5
    w1[...] = w_stage[0:16, :].astype(BF16)
    w1t[...] = w_stage[...].T[:, 0:16].astype(BF16)
    half_u = uw[...].astype(F32) * 0.5
    ew_row = ew[...].astype(F32)
    wue[...] = (half_u * ew_row).astype(BF16)
    wut[...] = half_u.T.astype(BF16)
    w_stage[0:C, :] = cw[...].astype(F32).T
    w_stage[C : C + 1, :] = ew_row
    w_stage[C + 1 : C + 2, :] = ew_row
    wct[...] = w_stage[0:80, :].astype(BF16)
    wcc[...] = w_stage[...].T[:, 0:80].astype(BF16)
    ew16[...] = jnp.broadcast_to(ew_row, (16, LAT)).astype(BF16)

    place_of = lax.broadcasted_iota(jnp.int32, (SPAN, ATOMS), 0)

    def mark(k, carry):
        place = nbr[0, 0, pl.ds(k, 1), :] & (SPAN - 1)
        onehot[k] = jnp.where(place_of == place, 1.0, 0.0).astype(BF16)
        return carry

    lax.fori_loop(0, K, mark, 0)

    for copy in sends:
        copy.wait_recv()

    row_of = lax.broadcasted_iota(jnp.int32, (8, BA), 0)

    def source(dr, dc):
        if (dr, dc) == (0, 0):
            return own
        return inbox.at[REACH.index((-dr, -dc))]

    def offset(x, y):
        return jnp.where(row_of == 0, x, 0.0) + jnp.where(row_of == 1, y, 0.0)

    def moved(block):
        return jnp.where(row_of == 3, pltpu.roll(block, 7, 0), block)

    centre = []
    for a in (-1, 0, 1):
        for b in (-1, 0, 1):
            x, y = SLAB * a, SLAB * b
            base = 16 * ((a + 1) * 3 + b + 1)
            tiles = [
                moved(source(a - 1, b)[:, BA:]) + offset(x - SLAB, y),
                moved(source(a, b - 1)[:, :BA]) + offset(x, y - SLAB),
                source(a, b)[:, :BA] + offset(x, y),
                source(a, b)[:, BA:] + offset(x, y),
            ]
            if (a, b) == (0, 0):
                centre = tiles
            for q, tile in enumerate(tiles):
                high = tile.astype(BF16)
                low = (tile - high.astype(F32)).astype(BF16)
                near_table[0, base + 8 * (q // 2) : base + 8 * (q // 2) + 8, BA * (q % 2) : BA * (q % 2) + BA] = high.astype(F32)
                near_table[1, base + 8 * (q // 2) : base + 8 * (q // 2) + 8, BA * (q % 2) : BA * (q % 2) + BA] = low.astype(F32)
    centre = jnp.concatenate(centre, axis=1)
    centre_xyz = jnp.where(lax.broadcasted_iota(jnp.int32, (8, ATOMS), 0) < 3, centre, 0.0)
    centre_code = centre[3:4, :]

    def gather(k, carry):
        group = jnp.broadcast_to(nbr[0, 0, pl.ds(k, 1), :] // SPAN, (8, ATOMS))
        hot = onehot[k]
        found = dot(near_table[0].astype(BF16), hot) + dot(near_table[1].astype(BF16), hot)
        picked = found[0:8]
        for g in range(1, GROUPS):
            picked = jnp.where(group == g, found[8 * g : 8 * g + 8], picked)
        picked = picked - centre_xyz
        for j in range(ATOMS // BA):
            rel_code[j, pl.ds(pl.multiple_of(8 * k, 8), 8), :] = picked[:, j * BA : j * BA + BA]
        return carry

    lax.fori_loop(0, K, gather, 0)

    rx, ry, rz, ncode = [
        jnp.concatenate([rel_code[j, pl.ds(c, K, stride=8), :] for j in range(ATOMS // BA)], axis=1)
        for c in range(4)
    ]
    live = jnp.where(jnp.logical_and(ncode > 0.5, centre_code > 0.5), 1.0, 0.0)
    sq = rx * rx + ry * ry + rz * rz
    cut = jnp.maximum(1.0 - sq * (1.0 / 64.0), 0.0)
    env = cut * cut * live
    ux, uy, uz = rx * SCALE, ry * SCALE, rz * SCALE
    norm = ux * ux + uy * uy + uz * uz
    for m, h in enumerate(
        [
            ux,
            uy,
            uz,
            ROOT3 * ux * uy,
            ROOT3 * uy * uz,
            0.5 * (3.0 * uz * uz - norm),
            ROOT3 * ux * uz,
            0.5 * ROOT3 * (ux * ux - uy * uy),
        ]
    ):
        harm[m + 1] = h
    edge[0] = sq
    edge[1] = env
    edge[2] = ncode

    row8 = lax.broadcasted_iota(jnp.int32, (8, ATOMS), 0)
    rates = jnp.zeros((8, ATOMS), F32)
    for n in range(8):
        rates = jnp.where(row8 == n, rate[n], rates)
    kind = jnp.where(row8 % 2 == 0, 1.0, 2.0)

    def first(k, carry):
        sq_k = edge[0, pl.ds(k, 1), :]
        env_k = edge[1, pl.ds(k, 1), :]
        basis = jnp.exp(-rates * sq_k) * env_k
        codes = jnp.where(row8 < 2, centre_code, edge[2, pl.ds(k, 1), :])
        hot = jnp.where(jnp.logical_and(codes == kind, row8 < 4), 1.0, 0.0)
        given = jnp.concatenate([basis, hot], axis=0).astype(BF16)
        for c in range(0, LAT, CHUNK):
            v = dot(w1t[c : c + CHUNK, :], given)
            t = jnp.tanh(v)
            vt = v * t
            latent[c : c + CHUNK, :] = (v + vt).astype(BF16)
            slope1[k, c : c + CHUNK, :] = ((1.0 + t) * ((1.0 + v) - vt)).astype(BF16)
        made = dot(wct[...], latent[...])
        mix0[k] = made[0:C]
        mix[k] = made[0:C] * env_k
        edge[3, pl.ds(k, 1), :] = made[C : C + 1]
        return carry

    lax.fori_loop(0, K, first, 0)

    def weigh(parts, source_of, out):
        for j in range(0, ATOMS, BA):
            for half in range(0, C, 32):
                total = [None] * 9
                for k in range(K):
                    read = [source_of(k, l, half, j) for l in range(parts)]
                    for m in range(9):
                        term = read[DEGREE[m] if parts == 3 else 0]
                        if m:
                            term = term * harm[m, k : k + 1, j : j + BA]
                        total[m] = term if k == 0 else total[m] + term
                for m in range(9):
                    out[m, half : half + 32, j : j + BA] = total[m] * NORM

    weigh(1, lambda k, l, half, j: mix[k, half : half + 32, j : j + BA], dens)

    def second(k, carry):
        env_k = edge[1, pl.ds(k, 1), :]
        h_rows = [None] + [harm[m, pl.ds(k, 1), :] for m in range(1, 9)]
        for j in range(0, ATOMS, BA):
            h = [None] + [h_rows[m][:, j : j + BA] for m in range(1, 9)]
            mixed = mix[k, :, j : j + BA]
            for l, terms in enumerate(([0], [1, 2, 3], [4, 5, 6, 7, 8])):
                prod = None
                for m in terms:
                    term = dens[m, :, j : j + BA]
                    if m:
                        term = term * h[m]
                    prod = term if prod is None else prod + term
                prods[l * C : l * C + C, j : j + BA] = prod
                scal[l * C : l * C + C, j : j + BA] = (prod * mixed).astype(BF16)
        for c in range(0, LAT, CHUNK):
            v = dot(wut[c : c + CHUNK, :], scal[...])
            t = jnp.tanh(v)
            vt = v * t
            updated[c : c + CHUNK, :] = (v + vt).astype(BF16)
            slope2[c : c + CHUNK, :] = ((1.0 + t) * ((1.0 + v) - vt)).astype(BF16)
        gain = dot(ew16[...], updated[...])
        edge[3, pl.ds(k, 1), :] = edge[3, pl.ds(k, 1), :] + gain[0:1]
        back = dot(wue[...], slope2[...])
        rows = [[] for _ in range(9)]
        for j in range(0, ATOMS, BA):
            env_j = env_k[:, j : j + BA]
            mixed = mix[k, :, j : j + BA]
            partial = None
            flows = []
            for l in range(3):
                flow = back[l * C : l * C + C, j : j + BA] * env_j
                term = flow * prods[l * C : l * C + C, j : j + BA]
                partial = term if partial is None else partial + term
                flow = flow * mixed
                dscal[k, l * C : l * C + C, j : j + BA] = flow
                flows.append(flow)
            dmix[k, :, j : j + BA] = partial
            for m in range(1, 9):
                rows[m].append(
                    jnp.sum(flows[DEGREE[m]] * dens[m, :, j : j + BA], axis=0, keepdims=True)
                )
        for m in range(1, 9):
            dharm[m, pl.ds(k, 1), :] = jnp.concatenate(rows[m], axis=1)
        return carry

    lax.fori_loop(0, K, second, 0)

    weigh(3, lambda k, l, half, j: dscal[k, l * C + half : l * C + half + 32, j : j + BA], ddens)

    def third(k, carry):
        sq_k = edge[0, pl.ds(k, 1), :]
        env_k = edge[1, pl.ds(k, 1), :]
        h_rows = [None] + [harm[m, pl.ds(k, 1), :] for m in range(1, 9)]
        rows = [[] for _ in range(9)]
        for j in range(0, ATOMS, BA):
            mixed = mix[k, :, j : j + BA]
            total = dmix[k, :, j : j + BA] + ddens[0, :, j : j + BA]
            for m in range(1, 9):
                slope = ddens[m, :, j : j + BA]
                total = total + slope * h_rows[m][:, j : j + BA]
                rows[m].append(jnp.sum(mixed * slope, axis=0, keepdims=True))
            rows[0].append(jnp.sum(total * mix0[k, :, j : j + BA], axis=0, keepdims=True))
            dlow[0:C, j : j + BA] = (total * env_k[:, j : j + BA]).astype(BF16)
        edge[4, pl.ds(k, 1), :] = jnp.concatenate(rows[0], axis=1)
        for m in range(1, 9):
            dharm[m, pl.ds(k, 1), :] = dharm[m, pl.ds(k, 1), :] + jnp.concatenate(rows[m], axis=1)
        high = env_k.astype(BF16).astype(F32)
        tail = jnp.where(
            lax.broadcasted_iota(jnp.int32, (16, ATOMS), 0) == 0,
            high,
            jnp.where(lax.broadcasted_iota(jnp.int32, (16, ATOMS), 0) == 1, env_k - high, 0.0),
        )
        dlow[C : C + 16, :] = tail.astype(BF16)
        for c in range(0, LAT, CHUNK):
            d = dot(wcc[c : c + CHUNK, :], dlow[...])
            dpre[c : c + CHUNK, :] = (d * slope1[k, c : c + CHUNK, :].astype(F32)).astype(BF16)
        db = dot(w1[...], dpre[...])[0:8]
        db = db * jnp.exp(-rates * sq_k)
        edge[5, pl.ds(k, 1), :] = jnp.sum(db, axis=0, keepdims=True)
        edge[6, pl.ds(k, 1), :] = jnp.sum(db * rates, axis=0, keepdims=True)
        return carry

    lax.fori_loop(0, K, third, 0)

    sums = edge[3]
    energies[0] = jnp.sum(sums * env, axis=0, keepdims=True)
    denv = sums + edge[4] + edge[5]
    dsq = (-edge[6]) * env + denv * live * cut * (-2.0 / 64.0)
    dh = [None] + [dharm[m] for m in range(1, 9)]
    gx = SCALE * (dh[1] + ROOT3 * (uy * dh[4] + uz * dh[7] + ux * dh[8]) - ux * dh[6]) + 2.0 * rx * dsq
    gy = SCALE * (dh[2] + ROOT3 * (ux * dh[4] + uz * dh[5] - uy * dh[8]) - uy * dh[6]) + 2.0 * ry * dsq
    gz = SCALE * (dh[3] + ROOT3 * (uy * dh[5] + ux * dh[7]) + 2.0 * uz * dh[6]) + 2.0 * rz * dsq
    grads = (gx, gy, gz)
    terms = [r * g for r in (rx, ry, rz) for g in grads] + list(grads)
    for v, term in enumerate(terms):
        for j in range(ATOMS // BA):
            vals[j, 8 * v : 8 * v + 8, :] = term[:, j * BA : j * BA + BA]
    vals[:, 96:128, :] = jnp.zeros((ATOMS // BA, 32, BA), F32)

    ghost[...] = jnp.zeros_like(ghost)

    def scatter(k, carry):
        group = jnp.broadcast_to(nbr[0, 0, pl.ds(k, 1), :] // SPAN, (16, ATOMS))
        term = jnp.concatenate(
            [vals[j, pl.ds(k, 16, stride=8), :] for j in range(ATOMS // BA)], axis=1
        )
        spread = jnp.concatenate(
            [jnp.where(group == g, term, 0.0).astype(BF16) for g in range(GROUPS)], axis=0
        )
        ghost[...] += dot_nt(spread, onehot[k]).reshape(9, 32, SPAN)
        return carry

    lax.fori_loop(0, K, scatter, 0)

    outs = []
    for slot, (dr, dc) in enumerate(NEAR):
        copy = pltpu.make_async_remote_copy(
            src_ref=ghost.at[(dr + 1) * 3 + dc + 1],
            dst_ref=ghost_in.at[slot],
            send_sem=send_out.at[slot],
            recv_sem=recv_out.at[slot],
            device_id=at(dr, dc),
            device_id_type=MESH,
        )
        copy.start()
        outs.append(copy)
    own_sums = jnp.concatenate([jnp.sum(t, axis=0, keepdims=True) for t in terms], axis=0)
    total = ghost[4]
    for slot, copy in enumerate(outs):
        copy.wait_recv()
        total = total + ghost_in[slot]
    total = jnp.concatenate([total[0:12], total[16:28]], axis=1)
    forces[0, 0] = own_sums[9:12] - total[9:12]
    virial[0, 0] = -0.5 * (own_sums[0:9] + total[0:9])
    for copy in sends + outs:
        copy.wait_send()


def solution(mesh):
    n_row, n_col = mesh.shape["row"], mesh.shape["col"]
    vmem = pl.BlockSpec(memory_space=pltpu.VMEM)
    smem = pl.BlockSpec(memory_space=pltpu.SMEM)

    def on_device(pos, spc, valid, rcount, ccount, nbr, rate, rw, ct, nt, cw, uw, ew):
        return pl.pallas_call(
            functools.partial(kernel, n_row, n_col),
            out_shape=(
                jax.ShapeDtypeStruct((1, 1, 3, ATOMS), F32),
                jax.ShapeDtypeStruct((1, 1, 9, ATOMS), F32),
                jax.ShapeDtypeStruct((1, 1, ATOMS), F32),
            ),
            in_specs=[vmem] * 6 + [smem] + [vmem] * 6,
            out_specs=(vmem, vmem, vmem),
            scratch_shapes=[
                pltpu.VMEM((8, 2 * BA), F32),
                pltpu.VMEM((len(REACH), 8, 2 * BA), F32),
                pltpu.VMEM((2, 8 * GROUPS, SPAN), F32),
                pltpu.VMEM((ATOMS // BA, 8 * K, BA), F32),
                pltpu.VMEM((K, SPAN, ATOMS), BF16),
                pltpu.VMEM((9, K, ATOMS), F32),
                pltpu.VMEM((8, K, ATOMS), F32),
                pltpu.VMEM((128, LAT), F32),
                pltpu.VMEM((LAT, 16), BF16),
                pltpu.VMEM((16, LAT), BF16),
                pltpu.VMEM((LAT, 3 * C), BF16),
                pltpu.VMEM((3 * C, LAT), BF16),
                pltpu.VMEM((80, LAT), BF16),
                pltpu.VMEM((LAT, 80), BF16),
                pltpu.VMEM((16, LAT), BF16),
                pltpu.VMEM((LAT, ATOMS), BF16),
                pltpu.VMEM((K, LAT, ATOMS), BF16),
                pltpu.VMEM((LAT, ATOMS), BF16),
                pltpu.VMEM((LAT, ATOMS), BF16),
                pltpu.VMEM((K, C, ATOMS), F32),
                pltpu.VMEM((K, C, ATOMS), F32),
                pltpu.VMEM((9, C, ATOMS), F32),
                pltpu.VMEM((9, C, ATOMS), F32),
                pltpu.VMEM((3 * C, ATOMS), F32),
                pltpu.VMEM((3 * C, ATOMS), BF16),
                pltpu.VMEM((K, 3 * C, ATOMS), F32),
                pltpu.VMEM((K, C, ATOMS), F32),
                pltpu.VMEM((9, K, ATOMS), F32),
                pltpu.VMEM((80, ATOMS), BF16),
                pltpu.VMEM((LAT, ATOMS), BF16),
                pltpu.VMEM((ATOMS // BA, 128, BA), F32),
                pltpu.VMEM((9, 32, SPAN), F32),
                pltpu.VMEM((8, 32, SPAN), F32),
                pltpu.SemaphoreType.DMA((len(REACH),)),
                pltpu.SemaphoreType.DMA((len(REACH),)),
                pltpu.SemaphoreType.DMA((len(NEAR),)),
                pltpu.SemaphoreType.DMA((len(NEAR),)),
            ],
            compiler_params=pltpu.CompilerParams(
                collective_id=0, has_side_effects=True, vmem_limit_bytes=48 * 1024 * 1024
            ),
        )(pos, spc, valid, rcount, ccount, nbr, rate, rw, ct, nt, cw, uw, ew.reshape(1, LAT))

    in_specs = (
        P("row", "col", None, None),
        P("row", "col", None),
        P("row", "col", None),
        P("row", "col"),
        P("row", "col"),
        P("row", "col", None, None),
    ) + (P(),) * 7
    out_specs = (P("row", "col", None, None), P("row", "col", None, None), P("row", "col", None))
    return jax.shard_map(on_device, mesh=mesh, in_specs=in_specs, out_specs=out_specs, check_vma=False)
```

time: 191 us -> 57.3 us (0.30)
  the two profiles are of different devices: /device:TPU:4 before, /device:TPU:2 now
where the time goes in v1:
time: 57.3 us; the launch traced here: 57 us
  Pallas kernels  49.4 us (86%)
  local copies, waits for them, and re-layouts  5.59 us (10%)
  between operations  2.06 us (4%)
    pallas_call x1, Pallas kernels, on_device(): pl.pallas_call(functools.partial(kernel, n_row, n_col), out_shape=(jax.Sh...  49.4 us
    unnamed x19, local copies, waits for them, and re-layouts  3.69 us
    pallas_call x2, local copies, waits for them, and re-layouts, on_device(): pl.pallas_call(functools.partial(kernel, n_row, n_col), out_shape=(jax.Sh...  1.23 us

profile of v1, /device:TPU:2, one launch (start us, length us, event | category | flops | bytes accessed | tf_op | source)
XLA Modules:
  0.0 57.0 jit_solution(1520550522255932736)
XLA Ops:
  0.6 0.0 copy-start
  2.0 0.7 %reshape.9.ew = bf16[1,512]{1,0:T(2,128)(2,1)S(1)} reshape(bf16[512]{0:T(512)(128)(2,1)} %param.25) | data formatting | bytes 2048 | tf_op jit(solution)/shard_map/reshape | solution.py:477
  2.7 0.7 %copy.16.pos = f32[1,1,3,256]{3,2,1,0:T(4,128)S(1)} copy(f32[1,1,3,256]{3,1,2,0:T(1,128)} %param.13) | data formatting | bytes 6144 | tf_op args[0]
  3.3 0.0 copy-start.2
  3.3 0.0 copy-start.3
  3.3 0.0 copy-start.4
  3.3 0.0 copy-start.5
  3.4 0.0 copy-start.7
  3.4 1.0 %copy.17.cw = bf16[512,64]{1,0:T(8,128)(2,1)S(1)} copy(bf16[512,64]{0,1:T(8,128)(2,1)} %param.23) | data formatting | bytes 131072 | tf_op args[10]
  4.4 0.0 copy-done
  4.4 0.0 copy-done.2
  4.4 0.0 copy-done.3
  4.4 0.0 copy-done.4
  4.4 0.0 copy-done.5
  4.4 0.0 copy-done.7
  4.4 0.0 copy-start.1
  4.5 0.7 %copy-done.1 = s32[1,1,8,512]{3,2,1,0:T(8,128)S(1)} copy-done((s32[1,1,8,512]{3,2,1,0:T(8,128)S(1)}, s32[1,1,8,512]{3,2,1,0:T(8,128)}, u32[]{:S(2)}) %copy-start.1) | copy-done | bytes 16408
  5.2 0.0 copy-start.6
  5.2 0.7 %copy-done.6 = s32[1,1,256]{2,1,0:T(1,128)S(1)} copy-done((s32[1,1,256]{2,1,0:T(1,128)S(1)}, s32[1,1,256]{2,1,0:T(1,128)}, u32[]{:S(2)}) %copy-start.6) | copy-done | bytes 1048
  5.8 49.4 %shard_map.148 = (f32[1,1,3,512]{3,2,1,0:T(4,128)S(1)}, f32[1,1,9,512]{3,2,1,0:T(8,128)S(1)}, f32[1,1,512]{2,1,0:T(1,128)S(1)}) custom-call(f32[1,1,3,256]{3,2,1,0:T(4,128)S(1)} %copy.16.pos, s32[1,1,256]{2,1,0:T(1,128)S(1)} %copy-done.5, s32[1,1,256]{2,1,0:T(1,128)S(1)} %copy-done.6, s32[1,1]{1,0:T(1,128)S(6)} %copy.21.rcount, s32[1,1]{1,0:T(1,128)S(6)} %copy.22.ccount, ...), custom_call_target="tpu_custom_call" | custom-call | tf_op jit(solution)/shard_map/pallas_call | solution.py:426
  55.2 0.6 %copy.18 = f32[1,1,3,512]{3,1,2,0:T(1,128)} copy(f32[1,1,3,512]{3,2,1,0:T(4,128)S(1)} %get-tuple-element.3) | data formatting | bytes 12288 | tf_op jit(solution)/shard_map/pallas_call | solution.py:426
  55.8 0.6 %copy.19 = f32[1,1,9,512]{3,1,2,0:T(1,128)} copy(f32[1,1,9,512]{3,2,1,0:T(8,128)S(1)} %get-tuple-element.4) | data formatting | bytes 36864 | tf_op jit(solution)/shard_map/pallas_call | solution.py:426
  56.5 0.6 %copy.23 = f32[1,1,512]{2,1,0:T(1,128)} copy(f32[1,1,512]{2,1,0:T(1,128)S(1)} %get-tuple-element.11) | data formatting | bytes 4096
Async XLA Ops:
  0.6 3.8 %copy-start = (bf16[192,512]{1,0:T(8,128)(2,1)S(1)}, bf16[192,512]{1,0:T(8,128)(2,1)}, u32[]{:S(2)}) copy-start(bf16[192,512]{1,0:T(8,128)(2,1)} %uw.1) | copy-start | bytes 589828
  3.3 1.1 %copy-start.2 = (bf16[8,512]{1,0:T(8,128)(2,1)S(1)}, bf16[8,512]{1,0:T(8,128)(2,1)}, u32[]{:S(2)}) copy-start(bf16[8,512]{1,0:T(8,128)(2,1)} %rw.1) | copy-start | bytes 24580
  3.3 1.1 %copy-start.3 = (bf16[2,512]{1,0:T(2,128)(2,1)S(1)}, bf16[2,512]{1,0:T(2,128)(2,1)}, u32[]{:S(2)}) copy-start(bf16[2,512]{1,0:T(2,128)(2,1)} %ct.1) | copy-start | bytes 6148
  3.3 1.1 %copy-start.4 = (bf16[2,512]{1,0:T(2,128)(2,1)S(1)}, bf16[2,512]{1,0:T(2,128)(2,1)}, u32[]{:S(2)}) copy-start(bf16[2,512]{1,0:T(2,128)(2,1)} %nt.1) | copy-start | bytes 6148
  3.3 1.1 %copy-start.5 = (s32[1,1,256]{2,1,0:T(1,128)S(1)}, s32[1,1,256]{2,1,0:T(1,128)}, u32[]{:S(2)}) copy-start(s32[1,1,256]{2,1,0:T(1,128)} %spc.1) | copy-start | bytes 3076
  3.4 1.1 %copy-start.7 = (f32[8]{0:T(128)S(1)}, f32[8]{0:T(128)}, u32[]{:S(2)}) copy-start(f32[8]{0:T(128)} %rate.1) | copy-start | bytes 100
  4.4 0.7 %copy-start.1 = (s32[1,1,8,512]{3,2,1,0:T(8,128)S(1)}, s32[1,1,8,512]{3,2,1,0:T(8,128)}, u32[]{:S(2)}) copy-start(s32[1,1,8,512]{3,2,1,0:T(8,128)} %nbr.1) | copy-start | bytes 49156
  5.2 0.7 %copy-start.6 = (s32[1,1,256]{2,1,0:T(1,128)S(1)}, s32[1,1,256]{2,1,0:T(1,128)}, u32[]{:S(2)}) copy-start(s32[1,1,256]{2,1,0:T(1,128)} %valid.1) | copy-start | bytes 3076

commit v2 on v1

v2 whole, which is shorter than its diff:
```python
import functools
import math

import jax
import jax.numpy as jnp
from jax import lax
from jax.experimental import pallas as pl
from jax.experimental.pallas import tpu as pltpu
from jax.sharding import PartitionSpec as P

K = 8
BA = 128
C = 64
LAT = 512
ATOMS = 512
SPAN = 256
GROUPS = 18
SLAB = 8.0
SCALE = 0.25
ROOT3 = math.sqrt(3.0)
NORM = 1.0 / math.sqrt(8.0)
F32 = jnp.float32
BF16 = jnp.bfloat16
MESH = pl.DeviceIdType.MESH

NEAR = [(a, b) for a in (-1, 0, 1) for b in (-1, 0, 1) if (a, b) != (0, 0)]
REACH = NEAR + [(2, b) for b in (-1, 0, 1)] + [(a, 2) for a in (-1, 0, 1)]
DEGREE = [0, 1, 1, 1, 2, 2, 2, 2, 2]
HALF = 256


def dot(a, b):
    return lax.dot_general(a, b, (((1,), (0,)), ((), ())), preferred_element_type=F32)


def dot_nt(a, b):
    return lax.dot_general(a, b, (((1,), (1,)), ((), ())), preferred_element_type=F32)


def kernel(
    n_row,
    n_col,
    pos,
    spc,
    valid,
    rcount,
    ccount,
    nbr,
    rate,
    rw,
    ct,
    nt,
    cw,
    uw,
    ew,
    result,
    pos_v,
    spc_v,
    valid_v,
    rcount_v,
    ccount_v,
    nbr_v,
    rate_v,
    rw_v,
    ct_v,
    nt_v,
    cw_v,
    uw_v,
    ew_v,
    load_sem,
    own,
    inbox,
    near_stage,
    near_table,
    rel_code,
    onehot,
    harm,
    edge,
    w_stage,
    w1t,
    w1,
    wut,
    wue,
    wct,
    wcc,
    ew_wide,
    given,
    latent,
    slope1,
    slope2,
    mix0,
    mix,
    dens,
    ddens,
    prods,
    scal,
    dscal,
    dmix,
    dharm,
    dlow,
    dpre,
    vals,
    ghost,
    ghost_in,
    send_in,
    recv_in,
    send_out,
    recv_out,
):
    row = lax.axis_index("row")
    col = lax.axis_index("col")

    def at(dr, dc):
        return (lax.rem(row + (dr + n_row), n_row), lax.rem(col + (dc + n_col), n_col))

    barrier = pltpu.get_barrier_semaphore()
    for dr, dc in REACH:
        pl.semaphore_signal(barrier, inc=1, device_id=at(-dr, -dc), device_id_type=MESH)

    loads = [
        pltpu.make_async_copy(there, here, load_sem.at[i])
        for i, (there, here) in enumerate(
            [
                (pos, pos_v),
                (spc, spc_v),
                (valid, valid_v),
                (rcount, rcount_v),
                (ccount, ccount_v),
                (nbr, nbr_v),
                (rate, rate_v),
                (rw, rw_v),
                (ct, ct_v),
                (nt, nt_v),
                (cw, cw_v),
                (uw, uw_v),
                (ew, ew_v),
            ]
        )
    ]
    for load in loads:
        load.start()
    for load in loads[:5]:
        load.wait()

    code = (valid_v[0] * (spc_v[0] + 1)).astype(F32)
    moves = jnp.concatenate(
        [
            jnp.where(jnp.broadcast_to(ccount_v[...], (1, BA)) > 0, 1.0, 0.0),
            jnp.where(jnp.broadcast_to(rcount_v[...], (1, BA)) > 0, 1.0, 0.0),
        ],
        axis=1,
    )
    for i in range(3):
        own[i : i + 1, :] = pos_v[0, i]
        own[i + 4 : i + 5, :] = pos_v[0, i]
    own[3:4, :] = code * moves
    own[7:8, :] = code * (1.0 - moves)
    pl.semaphore_wait(barrier, len(REACH))
    sends = []
    for slot, (dr, dc) in enumerate(REACH):
        copy = pltpu.make_async_remote_copy(
            src_ref=own,
            dst_ref=inbox.at[slot],
            send_sem=send_in.at[slot],
            recv_sem=recv_in.at[slot],
            device_id=at(dr, dc),
            device_id_type=MESH,
        )
        copy.start()
        sends.append(copy)

    for load in loads[5:]:
        load.wait()
    w_stage[...] = jnp.zeros_like(w_stage)
    w_stage[0:8, :] = rw_v[...].astype(F32) * 0.5
    w_stage[8:10, :] = ct_v[...].astype(F32) * 0.5
    w_stage[10:12, :] = nt_v[...].astype(F32) * 0.5
    w1[...] = w_stage[0:16, :].astype(BF16)
    w1t[...] = w_stage[...].T[:, 0:16].astype(BF16)
    half_u = uw_v[...].astype(F32) * 0.5
    ew_row = ew_v[...].astype(F32).reshape(1, LAT)
    wue[...] = (half_u * ew_row).astype(BF16)
    wut[...] = half_u.T.astype(BF16)
    w_stage[0:C, :] = cw_v[...].astype(F32)
    w_stage[C : C + 1, :] = ew_row
    w_stage[C + 1 : C + 2, :] = ew_row
    wct[...] = w_stage[0:80, :].astype(BF16)
    turned = w_stage[...].T
    wcc[...] = turned[:, 0:80].astype(BF16)
    ew_wide[...] = jnp.broadcast_to(turned[:, C : C + 1], (LAT, BA))

    place_of = lax.broadcasted_iota(jnp.int32, (SPAN, ATOMS), 0)

    for k in range(K):
        place = nbr_v[0, 0, k : k + 1, :] & (SPAN - 1)
        onehot[k] = jnp.where(place_of == place, 1.0, 0.0).astype(BF16)

    for copy in sends:
        copy.wait_recv()

    row_of = lax.broadcasted_iota(jnp.int32, (8, BA), 0)

    def source(dr, dc):
        if (dr, dc) == (0, 0):
            return own
        return inbox.at[REACH.index((-dr, -dc))]

    centre = None
    for p in range(9):
        a, b = p // 3 - 1, p % 3 - 1
        tiles = []
        for half, brought, dx, dy in (
            (0, source(a - 1, b)[:, BA:], -SLAB, 0.0),
            (1, source(a, b - 1)[:, :BA], 0.0, -SLAB),
        ):
            tile = jnp.where(row_of < 4, brought, source(a, b)[:, half * BA : half * BA + BA])
            shift = jnp.where(row_of == 4, SLAB * a, jnp.where(row_of == 5, SLAB * b, 0.0))
            shift = jnp.where(row_of == 0, SLAB * a + dx, jnp.where(row_of == 1, SLAB * b + dy, shift))
            tiles.append(tile + shift)
        tile = jnp.concatenate(tiles, axis=1)
        high = tile.astype(BF16).astype(F32)
        near_stage[8 * p : 8 * p + 8, :] = high
        near_stage[72 + 8 * p : 80 + 8 * p, :] = tile - high
        if p == 4:
            centre = jnp.concatenate([tile, pltpu.roll(tile, 4, 0)], axis=1)
    near_table[...] = near_stage[...].astype(BF16)
    row8 = lax.broadcasted_iota(jnp.int32, (8, ATOMS), 0)
    centre_xyz = jnp.where(row8 < 3, centre, 0.0)
    centre_code = centre[3:4, :]

    for k in range(K):
        index = jnp.broadcast_to(nbr_v[0, 0, k : k + 1, :], (8, ATOMS))
        block = lax.shift_right_logical(index, 9)
        found = dot(near_table[...], onehot[k])
        picked = found[0:8] + found[72:80]
        for p in range(1, 9):
            picked = jnp.where(block == p, found[8 * p : 8 * p + 8] + found[72 + 8 * p : 80 + 8 * p], picked)
        picked = jnp.where((index & SPAN) != 0, pltpu.roll(picked, 4, 0), picked) - centre_xyz
        for j in range(ATOMS // BA):
            rel_code[j, 8 * k : 8 * k + 8, :] = picked[:, j * BA : j * BA + BA]

    rx, ry, rz, ncode = [
        jnp.concatenate([rel_code[j, pl.ds(c, K, stride=8), :] for j in range(ATOMS // BA)], axis=1)
        for c in range(4)
    ]
    live = jnp.where(jnp.logical_and(ncode > 0.5, centre_code > 0.5), 1.0, 0.0)
    sq = rx * rx + ry * ry + rz * rz
    cut = jnp.maximum(1.0 - sq * (1.0 / 64.0), 0.0)
    env = cut * cut * live
    ux, uy, uz = rx * SCALE, ry * SCALE, rz * SCALE
    norm = ux * ux + uy * uy + uz * uz
    for m, h in enumerate(
        [
            ux,
            uy,
            uz,
            ROOT3 * ux * uy,
            ROOT3 * uy * uz,
            0.5 * (3.0 * uz * uz - norm),
            ROOT3 * ux * uz,
            0.5 * ROOT3 * (ux * ux - uy * uy),
        ]
    ):
        harm[m + 1] = h
    edge[0] = sq
    edge[1] = env
    edge[2] = ncode

    rates = jnp.zeros((8, ATOMS), F32)
    for n in range(8):
        rates = jnp.where(row8 == n, rate_v[n], rates)
    kind = jnp.where(row8 % 2 == 0, 1.0, 2.0)

    def first_chain(k, h):
        v = dot(w1t[...], given[k, :, h : h + HALF])
        t = jnp.tanh(v)
        vt = v * t
        latent[k, :, h : h + HALF] = (v + vt).astype(BF16)
        slope1[k, :, h : h + HALF] = ((1.0 + t) * ((1.0 + v) - vt)).astype(BF16)

    def first_mix(k, h):
        made = dot(wct[...], latent[k, :, h : h + HALF])
        mix0[k, :, h : h + HALF] = made[0:C]
        mix[k, :, h : h + HALF] = made[0:C] * edge[1, k : k + 1, h : h + HALF]
        edge[3, k : k + 1, h : h + HALF] = made[C : C + 1]

    for k in range(K):
        basis = jnp.exp(-rates * sq[k : k + 1, :]) * env[k : k + 1, :]
        codes = jnp.where(row8 < 2, centre_code, ncode[k : k + 1, :])
        hot = jnp.where(jnp.logical_and(codes == kind, row8 < 4), 1.0, 0.0)
        given[k] = jnp.concatenate([basis, hot], axis=0).astype(BF16)
    for step in range(K + 1):
        for h in (0, HALF):
            if step < K:
                first_chain(step, h)
            if step > 0:
                first_mix(step - 1, h)

    def weigh(parts, source_of, out):
        for j in range(0, ATOMS, BA):
            for half in range(0, C, 32):
                total = [None] * 9
                for k in range(K):
                    read = [source_of(k, l, half, j) for l in range(parts)]
                    for m in range(9):
                        term = read[DEGREE[m] if parts == 3 else 0]
                        if m:
                            term = term * harm[m, k : k + 1, j : j + BA]
                        total[m] = term if k == 0 else total[m] + term
                for m in range(9):
                    out[m, half : half + 32, j : j + BA] = total[m] * NORM

    weigh(1, lambda k, l, half, j: mix[k, half : half + 32, j : j + BA], dens)

    def second_in(k, j):
        h = [None] + [harm[m, k : k + 1, j : j + BA] for m in range(1, 9)]
        mixed = mix[k, :, j : j + BA]
        for l, terms in enumerate(([0], [1, 2, 3], [4, 5, 6, 7, 8])):
            prod = None
            for m in terms:
                term = dens[m, :, j : j + BA]
                if m:
                    term = term * h[m]
                prod = term if prod is None else prod + term
            prods[k, l * C : l * C + C, j : j + BA] = prod
            scal[k, l * C : l * C + C, j : j + BA] = (prod * mixed).astype(BF16)

    def second_chain(k, h):
        v = dot(wut[...], scal[k, :, h : h + HALF])
        t = jnp.tanh(v)
        vt = v * t
        updated = v + vt
        slope2[k, :, h : h + HALF] = ((1.0 + t) * ((1.0 + v) - vt)).astype(BF16)
        for j in range(0, HALF, BA):
            gain = jnp.sum(updated[:, j : j + BA] * ew_wide[...], axis=0, keepdims=True)
            edge[7, k : k + 1, h + j : h + j + BA] = gain

    def second_out(k, h):
        back = dot(wue[...], slope2[k, :, h : h + HALF])
        for j in range(0, HALF, BA):
            at_j = slice(h + j, h + j + BA)
            env_j = edge[1, k : k + 1, at_j]
            both = mix[k, :, at_j] * env_j
            partial = None
            for l in range(3):
                flow = back[l * C : l * C + C, j : j + BA]
                term = flow * prods[k, l * C : l * C + C, at_j]
                partial = term if partial is None else partial + term
                dscal[k, l * C : l * C + C, at_j] = flow * both
            dmix[k, :, at_j] = partial * env_j

    for step in range(-1, K + 1):
        for h in (0, HALF):
            if 0 <= step < K:
                second_chain(step, h)
            if step + 1 < K:
                second_in(step + 1, h)
                second_in(step + 1, h + BA)
            if step > 0:
                second_out(step - 1, h)

    weigh(3, lambda k, l, half, j: dscal[k, l * C + half : l * C + half + 32, j : j + BA], ddens)

    def fold(x):
        return jnp.sum(x.reshape(8, 8, BA), axis=0)

    def rows_of(parts):
        pairs = [
            jnp.where(row_of < 4, parts[i], parts[i + 4])
            + pltpu.roll(jnp.where(row_of < 4, parts[i + 4], parts[i]), 4, 0)
            for i in range(4)
        ]
        for size in (2, 1):
            pairs = [
                jnp.where(
                    row_of % (2 * size) < size,
                    pairs[i] + pltpu.roll(pairs[i], 8 - size, 0),
                    pairs[i + size] + pltpu.roll(pairs[i + size], size, 0),
                )
                for i in range(size)
            ]
        return pairs[0]

    def third_in(k, j):
        at_j = slice(j, j + BA)
        mixed = mix[k, :, at_j]
        flows = [dscal[k, l * C : l * C + C, at_j] for l in range(3)]
        total = dmix[k, :, at_j] + ddens[0, :, at_j]
        parts = []
        for m in range(1, 9):
            slope = ddens[m, :, at_j]
            total = total + slope * harm[m, k : k + 1, at_j]
            parts.append(fold(mixed * slope + flows[DEGREE[m]] * dens[m, :, at_j]))
        dharm[j // BA, 8 * k : 8 * k + 8, :] = rows_of(parts)
        edge[4, k : k + 1, at_j] = jnp.sum(total * mix0[k, :, at_j], axis=0, keepdims=True)
        dlow[k, 0:C, at_j] = (total * edge[1, k : k + 1, at_j]).astype(BF16)

    def third_chain(k, h):
        d = dot(wcc[...], dlow[k, :, h : h + HALF])
        dpre[k, :, h : h + HALF] = (d * slope1[k, :, h : h + HALF].astype(F32)).astype(BF16)

    def third_out(k, h):
        db = dot(w1[...], dpre[k, :, h : h + HALF])[0:8]
        db = db * jnp.exp(-rates[:, h : h + HALF] * edge[0, k : k + 1, h : h + HALF])
        edge[5, k : k + 1, h : h + HALF] = jnp.sum(db, axis=0, keepdims=True)
        edge[6, k : k + 1, h : h + HALF] = jnp.sum(db * rates[:, h : h + HALF], axis=0, keepdims=True)

    row16 = lax.broadcasted_iota(jnp.int32, (16, ATOMS), 0)
    for k in range(K):
        env_k = env[k : k + 1, :]
        high = env_k.astype(BF16).astype(F32)
        tail = jnp.where(row16 == 0, high, jnp.where(row16 == 1, env_k - high, 0.0))
        dlow[k, C : C + 16, :] = tail.astype(BF16)
    for step in range(-1, K + 1):
        for h in (0, HALF):
            if 0 <= step < K:
                third_chain(step, h)
            if step + 1 < K:
                third_in(step + 1, h)
                third_in(step + 1, h + BA)
            if step > 0:
                third_out(step - 1, h)

    sums = edge[3] + edge[7]
    result[12, :, :] = jnp.sum(sums * env, axis=0, keepdims=True)
    denv = sums + edge[4] + edge[5]
    dsq = (-edge[6]) * env + denv * live * cut * (-2.0 / 64.0)
    dh = [None] + [
        jnp.concatenate([dharm[j, pl.ds(m, K, stride=8), :] for j in range(ATOMS // BA)], axis=1)
        for m in range(8)
    ]
    gx = SCALE * (dh[1] + ROOT3 * (uy * dh[4] + uz * dh[7] + ux * dh[8]) - ux * dh[6]) + 2.0 * rx * dsq
    gy = SCALE * (dh[2] + ROOT3 * (ux * dh[4] + uz * dh[5] - uy * dh[8]) - uy * dh[6]) + 2.0 * ry * dsq
    gz = SCALE * (dh[3] + ROOT3 * (uy * dh[5] + ux * dh[7]) + 2.0 * uz * dh[6]) + 2.0 * rz * dsq
    grads = (gx, gy, gz)
    terms = [r * g for r in (rx, ry, rz) for g in grads] + list(grads)
    for v, term in enumerate(terms):
        for j in range(ATOMS // BA):
            vals[j, 8 * v : 8 * v + 8, :] = term[:, j * BA : j * BA + BA]
    vals[:, 96:128, :] = jnp.zeros((ATOMS // BA, 32, BA), F32)

    for k in range(K):
        group = jnp.broadcast_to(lax.shift_right_logical(nbr_v[0, 0, k : k + 1, :], 8), (8, ATOMS))
        term = jnp.concatenate(
            [vals[j, pl.ds(k, 16, stride=8), :] for j in range(ATOMS // BA)], axis=1
        )
        upper = term[0:8]
        lower = term[8:16] + pltpu.roll(term[8:16], 4, 0)
        later = group - jnp.where(row8 < 4, 0, 1)
        pieces = [jnp.where(group == g, upper, 0.0) for g in range(GROUPS)]
        pieces += [jnp.where(later == g, lower, 0.0) for g in range(0, GROUPS, 2)]
        spread = jnp.concatenate(pieces, axis=0).astype(BF16)
        found = dot_nt(spread, onehot[k])
        first_part = found[0:144].reshape(9, 16, SPAN)
        second_part = found[144:216].reshape(9, 8, SPAN)
        if k == 0:
            ghost[:, 0:16, :] = first_part
            ghost[:, 16:24, :] = second_part
        else:
            ghost[:, 0:16, :] += first_part
            ghost[:, 16:24, :] += second_part

    outs = []
    for slot, (dr, dc) in enumerate(NEAR):
        copy = pltpu.make_async_remote_copy(
            src_ref=ghost.at[(dr + 1) * 3 + dc + 1],
            dst_ref=ghost_in.at[slot],
            send_sem=send_out.at[slot],
            recv_sem=recv_out.at[slot],
            device_id=at(dr, dc),
            device_id_type=MESH,
        )
        copy.start()
        outs.append(copy)
    own_sums = jnp.concatenate([jnp.sum(t, axis=0, keepdims=True) for t in terms], axis=0)
    total = ghost[4]
    for slot, copy in enumerate(outs):
        copy.wait_recv()
        total = total + ghost_in[slot]
    total = jnp.concatenate(
        [
            jnp.concatenate([total[0:8], total[16:20]], axis=0),
            jnp.concatenate([total[8:16], total[20:24]], axis=0),
        ],
        axis=1,
    )
    total = jnp.where(
        lax.broadcasted_iota(jnp.int32, (12, ATOMS), 0) < 9,
        -0.5 * (own_sums + total),
        own_sums - total,
    )
    for v in range(12):
        result[v, :, :] = total[v : v + 1]
    for copy in sends + outs:
        copy.wait_send()


def share_out(result, forces, virial, energies):
    virial[...] = result[0:9]
    forces[...] = result[9:12]
    energies[...] = result[12:13]


def solution(mesh):
    n_row, n_col = mesh.shape["row"], mesh.shape["col"]
    hbm = pl.BlockSpec(memory_space=pltpu.HBM)

    def on_device(pos, spc, valid, rcount, ccount, nbr, rate, rw, ct, nt, cw, uw, ew):
        args = (pos.transpose(0, 2, 1, 3), spc, valid, rcount, ccount, nbr, rate, rw, ct, nt, cw.T, uw, ew)
        held = [pltpu.VMEM(a.shape, a.dtype) for a in args]
        held[6] = pltpu.SMEM(rate.shape, rate.dtype)
        result = pl.pallas_call(
            functools.partial(kernel, n_row, n_col),
            out_shape=jax.ShapeDtypeStruct((13, 1, ATOMS), F32),
            in_specs=[hbm] * len(args),
            out_specs=pl.BlockSpec(memory_space=pltpu.VMEM),
            scratch_shapes=held
            + [
                pltpu.SemaphoreType.DMA((13,)),
                pltpu.VMEM((8, 2 * BA), F32),
                pltpu.VMEM((len(REACH), 8, 2 * BA), F32),
                pltpu.VMEM((144, SPAN), F32),
                pltpu.VMEM((144, SPAN), BF16),
                pltpu.VMEM((ATOMS // BA, 8 * K, BA), F32),
                pltpu.VMEM((K, SPAN, ATOMS), BF16),
                pltpu.VMEM((9, K, ATOMS), F32),
                pltpu.VMEM((8, K, ATOMS), F32),
                pltpu.VMEM((128, LAT), F32),
                pltpu.VMEM((LAT, 16), BF16),
                pltpu.VMEM((16, LAT), BF16),
                pltpu.VMEM((LAT, 3 * C), BF16),
                pltpu.VMEM((3 * C, LAT), BF16),
                pltpu.VMEM((80, LAT), BF16),
                pltpu.VMEM((LAT, 80), BF16),
                pltpu.VMEM((LAT, BA), F32),
                pltpu.VMEM((K, 16, ATOMS), BF16),
                pltpu.VMEM((K, LAT, ATOMS), BF16),
                pltpu.VMEM((K, LAT, ATOMS), BF16),
                pltpu.VMEM((K, LAT, ATOMS), BF16),
                pltpu.VMEM((K, C, ATOMS), F32),
                pltpu.VMEM((K, C, ATOMS), F32),
                pltpu.VMEM((9, C, ATOMS), F32),
                pltpu.VMEM((9, C, ATOMS), F32),
                pltpu.VMEM((K, 3 * C, ATOMS), F32),
                pltpu.VMEM((K, 3 * C, ATOMS), BF16),
                pltpu.VMEM((K, 3 * C, ATOMS), F32),
                pltpu.VMEM((K, C, ATOMS), F32),
                pltpu.VMEM((ATOMS // BA, 8 * K, BA), F32),
                pltpu.VMEM((K, 80, ATOMS), BF16),
                pltpu.VMEM((K, LAT, ATOMS), BF16),
                pltpu.VMEM((ATOMS // BA, 128, BA), F32),
                pltpu.VMEM((9, 24, SPAN), F32),
                pltpu.VMEM((8, 24, SPAN), F32),
                pltpu.SemaphoreType.DMA((len(REACH),)),
                pltpu.SemaphoreType.DMA((len(REACH),)),
                pltpu.SemaphoreType.DMA((len(NEAR),)),
                pltpu.SemaphoreType.DMA((len(NEAR),)),
            ],
            compiler_params=pltpu.CompilerParams(
                collective_id=0, has_side_effects=True, vmem_limit_bytes=64 * 1024 * 1024
            ),
        )(*args)
        forces, virial, energies = pl.pallas_call(
            share_out,
            out_shape=[jax.ShapeDtypeStruct((n, 1, ATOMS), F32) for n in (3, 9, 1)],
            in_specs=[pl.BlockSpec(memory_space=pltpu.VMEM)],
            out_specs=[pl.BlockSpec(memory_space=pltpu.VMEM)] * 3,
            compiler_params=pltpu.CompilerParams(vmem_limit_bytes=1 << 20),
        )(result)
        return (
            forces.reshape(1, 3, 1, ATOMS).transpose(0, 2, 1, 3),
            virial.reshape(1, 9, 1, ATOMS).transpose(0, 2, 1, 3),
            energies,
        )

    in_specs = (
        P("row", "col", None, None),
        P("row", "col", None),
        P("row", "col", None),
        P("row", "col"),
        P("row", "col"),
        P("row", "col", None, None),
    ) + (P(),) * 7
    out_specs = (P("row", "col", None, None), P("row", "col", None, None), P("row", "col", None))
    return jax.shard_map(on_device, mesh=mesh, in_specs=in_specs, out_specs=out_specs, check_vma=False)
```

time: 57.3 us -> 44.5 us (0.78)
  Pallas kernels: 49.4 us -> 41.7 us
  local copies, waits for them, and re-layouts: 5.59 us -> 0.74 us
    pallas_call x1 -> x2, Pallas kernels: 49.4 us -> 41.7 us  [the longest x1 41 us: on_device(): pl.pallas_call(functools.partial(kernel, n_row, n_col), out_shape=jax.Sha...]
    unnamed x19 -> x2, local copies, waits for them, and re-layouts: 3.69 us -> 0.74 us
    pallas_call x2 -> x0, local copies, waits for them, and re-layouts: 1.23 us -> none  [on_device(): pl.pallas_call(functools.partial(kernel, n_row, n_col), out_shape=(jax.Sh...]
    reshape x1 -> x0, local copies, waits for them, and re-layouts: 0.68 us -> none  [on_device(): ew.reshape(1, LAT)]
where the time goes in v2:
time: 44.5 us; the launch traced here: 44.3 us
  Pallas kernels  41.7 us (94%)
  between operations  1.94 us (4%)
  local copies, waits for them, and re-layouts  0.74 us (2%)
    pallas_call x1, Pallas kernels, on_device(): pl.pallas_call(functools.partial(kernel, n_row, n_col), out_shape=jax.Sha...  41 us

profile of v2, /device:TPU:2, one launch (start us, length us, event | category | flops | bytes accessed | tf_op | source)
XLA Modules:
  0.0 44.3 jit_solution(6933818716397659298)
XLA Ops:
  1.9 41.0 %shard_map.148.result = f32[13,1,512]{2,1,0:T(1,128)} custom-call(f32[1,3,1,256]{3,2,1,0:T(1,128)} %bitcast.9, s32[1,1,256]{2,1,0:T(1,128)} %spc.1, s32[1,1,256]{2,1,0:T(1,128)} %valid.1, s32[1,1]{1,0:T(1,128)S(6)} %copy.18.rcount, s32[1,1]{1,0:T(1,128)S(6)} %copy.19.ccount, s32[1,1,8,512]{3,2,1,0:T(8,128)} %nbr.1, f32[8]{0:T(128)} %rate.1, ...), custom_call_target="tpu_custom_call" | custom-call | tf_op jit(solution)/shard_map/pallas_call | solution.py:512
  43.0 0.0 copy-start
  43.0 0.7 %copy-done = f32[13,1,512]{2,1,0:T(1,128)S(1)} copy-done((f32[13,1,512]{2,1,0:T(1,128)S(1)}, f32[13,1,512]{2,1,0:T(1,128)}, u32[]{:S(2)}) %copy-start) | copy-done | bytes 26648
  43.7 0.6 %shard_map.149 = (f32[3,1,512]{2,1,0:T(1,128)}, f32[9,1,512]{2,1,0:T(1,128)}, f32[1,1,512]{2,1,0:T(1,128)}) custom-call(f32[13,1,512]{2,1,0:T(1,128)S(1)} %copy-done), custom_call_target="tpu_custom_call" | custom-call | tf_op jit(solution)/shard_map/pallas_call | solution.py:563
Async XLA Ops:
  43.0 0.7 %copy-start = (f32[13,1,512]{2,1,0:T(1,128)S(1)}, f32[13,1,512]{2,1,0:T(1,128)}, u32[]{:S(2)}) copy-start(f32[13,1,512]{2,1,0:T(1,128)} %shard_map.148.result) | copy-start | bytes 79876

commit v3 on v2

--- a/solution.py
+++ b/solution.py
@@ -27,14 +27,13 @@
 REACH = NEAR + [(2, b) for b in (-1, 0, 1)] + [(a, 2) for a in (-1, 0, 1)]
 DEGREE = [0, 1, 1, 1, 2, 2, 2, 2, 2]
 HALF = 256
+STRIP = 16
+ROWS = 64
+BITE = 32
 
 
 def dot(a, b):
     return lax.dot_general(a, b, (((1,), (0,)), ((), ())), preferred_element_type=F32)
-
-
-def dot_nt(a, b):
-    return lax.dot_general(a, b, (((1,), (1,)), ((), ())), preferred_element_type=F32)
 
 
 def kernel(
@@ -74,8 +73,10 @@
     near_table,
     rel_code,
     onehot,
+    turned_hot,
     harm,
     edge,
+    wide_env,
     w_stage,
     w1t,
     w1,
@@ -97,6 +98,11 @@
     dscal,
     dmix,
     dharm,
+    folded,
+    gain1,
+    gain2,
+    gain3,
+    dbasis,
     dlow,
     dpre,
     vals,
@@ -112,10 +118,6 @@
 
     def at(dr, dc):
         return (lax.rem(row + (dr + n_row), n_row), lax.rem(col + (dc + n_col), n_col))
-
-    barrier = pltpu.get_barrier_semaphore()
-    for dr, dc in REACH:
-        pl.semaphore_signal(barrier, inc=1, device_id=at(-dr, -dc), device_id_type=MESH)
 
     loads = [
         pltpu.make_async_copy(there, here, load_sem.at[i])
@@ -137,7 +139,12 @@
             ]
         )
     ]
-    for load in loads:
+    for load in loads[:5]:
+        load.start()
+    barrier = pltpu.get_barrier_semaphore()
+    for dr, dc in REACH:
+        pl.semaphore_signal(barrier, inc=1, device_id=at(-dr, -dc), device_id_type=MESH)
+    for load in loads[5:]:
         load.start()
     for load in loads[:5]:
         load.wait()
@@ -150,11 +157,12 @@
         ],
         axis=1,
     )
-    for i in range(3):
-        own[i : i + 1, :] = pos_v[0, i]
-        own[i + 4 : i + 5, :] = pos_v[0, i]
-    own[3:4, :] = code * moves
-    own[7:8, :] = code * (1.0 - moves)
+    code = code * (1.0 - 2.0 * moves)
+    for half in range(2):
+        at_half = slice(half * BA, half * BA + BA)
+        for i in range(3):
+            own[4 * half + i : 4 * half + i + 1, :] = pos_v[0, i][:, at_half]
+        own[4 * half + 3 : 4 * half + 4, :] = code[:, at_half]
     pl.semaphore_wait(barrier, len(REACH))
     sends = []
     for slot, (dr, dc) in enumerate(REACH):
@@ -193,7 +201,9 @@
 
     for k in range(K):
         place = nbr_v[0, 0, k : k + 1, :] & (SPAN - 1)
-        onehot[k] = jnp.where(place_of == place, 1.0, 0.0).astype(BF16)
+        marks = jnp.where(place_of == place, 1.0, 0.0)
+        onehot[k] = marks.astype(BF16)
+        turned_hot[k] = marks.T.astype(BF16)
 
     for copy in sends:
         copy.wait_recv()
@@ -208,12 +218,14 @@
     centre = None
     for p in range(9):
         a, b = p // 3 - 1, p % 3 - 1
+        here = source(a, b)[...]
         tiles = []
-        for half, brought, dx, dy in (
-            (0, source(a - 1, b)[:, BA:], -SLAB, 0.0),
-            (1, source(a, b - 1)[:, :BA], 0.0, -SLAB),
+        for tile, dx, dy in (
+            (pltpu.roll(jnp.where(row_of < 4, here, source(a - 1, b)[...]), 4, 0), -SLAB, 0.0),
+            (jnp.where(row_of < 4, source(a, b - 1)[...], here), 0.0, -SLAB),
         ):
-            tile = jnp.where(row_of < 4, brought, source(a, b)[:, half * BA : half * BA + BA])
+            tile = jnp.where(row_of == 3, jnp.maximum(-tile, 0.0), tile)
+            tile = jnp.where(row_of == 7, jnp.maximum(tile, 0.0), tile)
             shift = jnp.where(row_of == 4, SLAB * a, jnp.where(row_of == 5, SLAB * b, 0.0))
             shift = jnp.where(row_of == 0, SLAB * a + dx, jnp.where(row_of == 1, SLAB * b + dy, shift))
             tiles.append(tile + shift)
@@ -261,7 +273,10 @@
             0.5 * ROOT3 * (ux * ux - uy * uy),
         ]
     ):
-        harm[m + 1] = h
+        for k in range(K):
+            harm[m, k] = jnp.broadcast_to(h[k : k + 1, :], (8, ATOMS))
+    for k in range(K):
+        wide_env[k] = jnp.broadcast_to(env[k : k + 1, :], (8, ATOMS))
     edge[0] = sq
     edge[1] = env
     edge[2] = ncode
@@ -271,111 +286,140 @@
         rates = jnp.where(row8 == n, rate_v[n], rates)
     kind = jnp.where(row8 % 2 == 0, 1.0, 2.0)
 
-    def first_chain(k, h):
-        v = dot(w1t[...], given[k, :, h : h + HALF])
-        t = jnp.tanh(v)
-        vt = v * t
-        latent[k, :, h : h + HALF] = (v + vt).astype(BF16)
-        slope1[k, :, h : h + HALF] = ((1.0 + t) * ((1.0 + v) - vt)).astype(BF16)
+    def fold(x):
+        return jnp.sum(x.reshape(x.shape[0] // 8, 8, BA), axis=0)
+
+    def by_row(x, rows):
+        return (x.reshape(x.shape[0] // 8, 8, x.shape[1]) * rows[None]).reshape(x.shape)
+
+    pieces = [(k, h) for k in range(K) for h in (0, HALF)]
+
+    def pipeline(prepare, start, chain, finish, end):
+        begun, left, n = {}, {}, len(pieces)
+        for t in range(-2, n + 1):
+            if 0 <= t + 1 < n:
+                begun[t + 1] = start(*pieces[t + 1])
+            if 0 <= t - 1 < n:
+                left[t - 1] = finish(*pieces[t - 1])
+            if 0 <= t < n:
+                chain(*pieces[t], begun.pop(t))
+            if 0 <= t - 1 < n:
+                end(*pieces[t - 1], left.pop(t - 1))
+            if 0 <= t + 2 < n and prepare is not None:
+                prepare(*pieces[t + 2])
+
+    def first_start(k, h):
+        return dot(w1t[...], given[k, :, h : h + HALF])
+
+    def first_chain(k, h, v):
+        for c in range(0, LAT, ROWS):
+            part = v[c : c + ROWS]
+            t = jnp.tanh(part)
+            vt = part * t
+            latent[k, c : c + ROWS, h : h + HALF] = (part + vt).astype(BF16)
+            slope1[k, c : c + ROWS, h : h + HALF] = ((1.0 + t) * ((1.0 + part) - vt)).astype(BF16)
 
     def first_mix(k, h):
-        made = dot(wct[...], latent[k, :, h : h + HALF])
+        return dot(wct[...], latent[k, :, h : h + HALF])
+
+    def first_end(k, h, made):
         mix0[k, :, h : h + HALF] = made[0:C]
-        mix[k, :, h : h + HALF] = made[0:C] * edge[1, k : k + 1, h : h + HALF]
-        edge[3, k : k + 1, h : h + HALF] = made[C : C + 1]
+        mix[k, :, h : h + HALF] = by_row(made[0:C], wide_env[k, :, h : h + HALF])
+        gain1[k, :, h : h + HALF] = made[C : C + 8]
 
     for k in range(K):
         basis = jnp.exp(-rates * sq[k : k + 1, :]) * env[k : k + 1, :]
         codes = jnp.where(row8 < 2, centre_code, ncode[k : k + 1, :])
         hot = jnp.where(jnp.logical_and(codes == kind, row8 < 4), 1.0, 0.0)
         given[k] = jnp.concatenate([basis, hot], axis=0).astype(BF16)
-    for step in range(K + 1):
-        for h in (0, HALF):
-            if step < K:
-                first_chain(step, h)
-            if step > 0:
-                first_mix(step - 1, h)
+    pipeline(None, first_start, first_chain, first_mix, first_end)
 
     def weigh(parts, source_of, out):
         for j in range(0, ATOMS, BA):
-            for half in range(0, C, 32):
+            for c in range(0, C, STRIP):
                 total = [None] * 9
                 for k in range(K):
-                    read = [source_of(k, l, half, j) for l in range(parts)]
+                    read = [source_of(k, l, c, j) for l in range(parts)]
                     for m in range(9):
                         term = read[DEGREE[m] if parts == 3 else 0]
                         if m:
-                            term = term * harm[m, k : k + 1, j : j + BA]
+                            term = by_row(term, harm[m - 1, k, :, j : j + BA])
                         total[m] = term if k == 0 else total[m] + term
                 for m in range(9):
-                    out[m, half : half + 32, j : j + BA] = total[m] * NORM
-
-    weigh(1, lambda k, l, half, j: mix[k, half : half + 32, j : j + BA], dens)
+                    out[m, c : c + STRIP, j : j + BA] = total[m] * NORM
+
+    weigh(1, lambda k, l, c, j: mix[k, c : c + STRIP, j : j + BA], dens)
 
     def second_in(k, j):
-        h = [None] + [harm[m, k : k + 1, j : j + BA] for m in range(1, 9)]
+        h = [None] + [harm[m, k, :, j : j + BA] for m in range(8)]
         mixed = mix[k, :, j : j + BA]
         for l, terms in enumerate(([0], [1, 2, 3], [4, 5, 6, 7, 8])):
             prod = None
             for m in terms:
                 term = dens[m, :, j : j + BA]
                 if m:
-                    term = term * h[m]
+                    term = by_row(term, h[m])
                 prod = term if prod is None else prod + term
             prods[k, l * C : l * C + C, j : j + BA] = prod
             scal[k, l * C : l * C + C, j : j + BA] = (prod * mixed).astype(BF16)
 
-    def second_chain(k, h):
-        v = dot(wut[...], scal[k, :, h : h + HALF])
-        t = jnp.tanh(v)
-        vt = v * t
-        updated = v + vt
-        slope2[k, :, h : h + HALF] = ((1.0 + t) * ((1.0 + v) - vt)).astype(BF16)
-        for j in range(0, HALF, BA):
-            gain = jnp.sum(updated[:, j : j + BA] * ew_wide[...], axis=0, keepdims=True)
-            edge[7, k : k + 1, h + j : h + j + BA] = gain
-
-    def second_out(k, h):
-        back = dot(wue[...], slope2[k, :, h : h + HALF])
+    def second_prepare(k, h):
+        second_in(k, h)
+        second_in(k, h + BA)
+
+    def second_start(k, h):
+        return dot(wut[...], scal[k, :, h : h + HALF])
+
+    def second_chain(k, h, v):
+        gains = [0.0] * (HALF // BA)
+        for c in range(0, LAT, ROWS):
+            part = v[c : c + ROWS]
+            t = jnp.tanh(part)
+            vt = part * t
+            updated = part + vt
+            slope2[k, c : c + ROWS, h : h + HALF] = ((1.0 + t) * ((1.0 + part) - vt)).astype(BF16)
+            weight = ew_wide[c : c + ROWS, :]
+            for j in range(HALF // BA):
+                gain = updated[:, j * BA : j * BA + BA] * weight
+                gains[j] = gains[j] + fold(gain)
+        for j in range(HALF // BA):
+            gain2[k, :, h + j * BA : h + j * BA + BA] = gains[j]
+
+    def second_back(k, h):
+        return dot(wue[...], slope2[k, :, h : h + HALF])
+
+    def second_end(k, h, back):
         for j in range(0, HALF, BA):
             at_j = slice(h + j, h + j + BA)
-            env_j = edge[1, k : k + 1, at_j]
-            both = mix[k, :, at_j] * env_j
+            env_j = wide_env[k, :, at_j]
+            both = by_row(mix[k, :, at_j], env_j)
             partial = None
             for l in range(3):
                 flow = back[l * C : l * C + C, j : j + BA]
                 term = flow * prods[k, l * C : l * C + C, at_j]
                 partial = term if partial is None else partial + term
                 dscal[k, l * C : l * C + C, at_j] = flow * both
-            dmix[k, :, at_j] = partial * env_j
-
-    for step in range(-1, K + 1):
-        for h in (0, HALF):
-            if 0 <= step < K:
-                second_chain(step, h)
-            if step + 1 < K:
-                second_in(step + 1, h)
-                second_in(step + 1, h + BA)
-            if step > 0:
-                second_out(step - 1, h)
-
-    weigh(3, lambda k, l, half, j: dscal[k, l * C + half : l * C + half + 32, j : j + BA], ddens)
-
-    def fold(x):
-        return jnp.sum(x.reshape(8, 8, BA), axis=0)
+            dmix[k, :, at_j] = by_row(partial, env_j)
+
+    pipeline(second_prepare, second_start, second_chain, second_back, second_end)
+
+    weigh(3, lambda k, l, c, j: dscal[k, l * C + c : l * C + c + STRIP, j : j + BA], ddens)
+
+    row_in = lax.broadcasted_iota(jnp.int32, (4 * K, 8, BA), 1)
+    masks = [row_in < 4, (row_in & 2) == 0, (row_in & 1) == 0]
 
     def rows_of(parts):
         pairs = [
-            jnp.where(row_of < 4, parts[i], parts[i + 4])
-            + pltpu.roll(jnp.where(row_of < 4, parts[i + 4], parts[i]), 4, 0)
+            jnp.where(masks[0], parts[i], parts[i + 4])
+            + pltpu.roll(jnp.where(masks[0], parts[i + 4], parts[i]), 4, 1)
             for i in range(4)
         ]
         for size in (2, 1):
             pairs = [
                 jnp.where(
-                    row_of % (2 * size) < size,
-                    pairs[i] + pltpu.roll(pairs[i], 8 - size, 0),
-                    pairs[i + size] + pltpu.roll(pairs[i + size], size, 0),
+                    masks[3 - size],
+                    pairs[i] + pltpu.roll(pairs[i], 8 - size, 1),
+                    pairs[i + size] + pltpu.roll(pairs[i + size], size, 1),
                 )
                 for i in range(size)
             ]
@@ -383,27 +427,41 @@
 
     def third_in(k, j):
         at_j = slice(j, j + BA)
-        mixed = mix[k, :, at_j]
-        flows = [dscal[k, l * C : l * C + C, at_j] for l in range(3)]
-        total = dmix[k, :, at_j] + ddens[0, :, at_j]
-        parts = []
-        for m in range(1, 9):
-            slope = ddens[m, :, at_j]
-            total = total + slope * harm[m, k : k + 1, at_j]
-            parts.append(fold(mixed * slope + flows[DEGREE[m]] * dens[m, :, at_j]))
-        dharm[j // BA, 8 * k : 8 * k + 8, :] = rows_of(parts)
-        edge[4, k : k + 1, at_j] = jnp.sum(total * mix0[k, :, at_j], axis=0, keepdims=True)
-        dlow[k, 0:C, at_j] = (total * edge[1, k : k + 1, at_j]).astype(BF16)
-
-    def third_chain(k, h):
-        d = dot(wcc[...], dlow[k, :, h : h + HALF])
-        dpre[k, :, h : h + HALF] = (d * slope1[k, :, h : h + HALF].astype(F32)).astype(BF16)
-
-    def third_out(k, h):
-        db = dot(w1[...], dpre[k, :, h : h + HALF])[0:8]
-        db = db * jnp.exp(-rates[:, h : h + HALF] * edge[0, k : k + 1, h : h + HALF])
-        edge[5, k : k + 1, h : h + HALF] = jnp.sum(db, axis=0, keepdims=True)
-        edge[6, k : k + 1, h : h + HALF] = jnp.sum(db * rates[:, h : h + HALF], axis=0, keepdims=True)
+        parts = [0.0] * 8
+        pull = 0.0
+        for c in range(0, C, BITE):
+            at_c = slice(c, c + BITE)
+            mixed = mix[k, at_c, at_j]
+            flows = [dscal[k, l * C + c : l * C + c + BITE, at_j] for l in range(3)]
+            total = dmix[k, at_c, at_j] + ddens[0, at_c, at_j]
+            for m in range(1, 9):
+                slope = ddens[m, at_c, at_j]
+                total = total + by_row(slope, harm[m - 1, k, :, at_j])
+                parts[m - 1] = parts[m - 1] + fold(mixed * slope + flows[DEGREE[m]] * dens[m, at_c, at_j])
+            pull = pull + fold(total * mix0[k, at_c, at_j])
+            dlow[k, at_c, at_j] = by_row(total, wide_env[k, :, at_j]).astype(BF16)
+        for m in range(8):
+            folded[m, K * (j // BA) + k] = parts[m]
+        gain3[k, :, at_j] = pull
+
+    def third_prepare(k, h):
+        third_in(k, h)
+        third_in(k, h + BA)
+
+    def third_start(k, h):
+        return dot(wcc[...], dlow[k, :, h : h + HALF])
+
+    def third_chain(k, h, d):
+        for c in range(0, LAT, ROWS):
+            part = d[c : c + ROWS] * slope1[k, c : c + ROWS, h : h + HALF].astype(F32)
+            dpre[k, c : c + ROWS, h : h + HALF] = part.astype(BF16)
+
+    def third_back(k, h):
+        return dot(w1[...], dpre[k, :, h : h + HALF])
+
+    def third_end(k, h, db):
+        db = db[0:8] * jnp.exp(-rates[:, h : h + HALF] * edge[0, k : k + 1, h : h + HALF])
+        dbasis[k, :, h : h + HALF] = db
 
     row16 = lax.broadcasted_iota(jnp.int32, (16, ATOMS), 0)
     for k in range(K):
@@ -411,20 +469,18 @@
         high = env_k.astype(BF16).astype(F32)
         tail = jnp.where(row16 == 0, high, jnp.where(row16 == 1, env_k - high, 0.0))
         dlow[k, C : C + 16, :] = tail.astype(BF16)
-    for step in range(-1, K + 1):
-        for h in (0, HALF):
-            if 0 <= step < K:
-                third_chain(step, h)
-            if step + 1 < K:
-                third_in(step + 1, h)
-                third_in(step + 1, h + BA)
-            if step > 0:
-                third_out(step - 1, h)
-
-    sums = edge[3] + edge[7]
+    pipeline(third_prepare, third_start, third_chain, third_back, third_end)
+
+    turned_rows = rows_of([folded[m] for m in range(8)]).reshape(ATOMS // BA, 8 * K, BA)
+    dharm[...] = turned_rows
+    top = lax.broadcasted_iota(jnp.int32, (K, 8, ATOMS), 1) == 0
+    sums = jnp.sum(gain2[...] + jnp.where(top, gain1[...], 0.0), axis=1)
+    back_rows = dbasis[...]
+    pulled = jnp.sum(gain3[...] + back_rows, axis=1)
+    shrunk = jnp.sum(back_rows * rates[None], axis=1)
     result[12, :, :] = jnp.sum(sums * env, axis=0, keepdims=True)
-    denv = sums + edge[4] + edge[5]
-    dsq = (-edge[6]) * env + denv * live * cut * (-2.0 / 64.0)
+    denv = sums + pulled
+    dsq = -shrunk * env + denv * live * cut * (-2.0 / 64.0)
     dh = [None] + [
         jnp.concatenate([dharm[j, pl.ds(m, K, stride=8), :] for j in range(ATOMS // BA)], axis=1)
         for m in range(8)
@@ -450,7 +506,7 @@
         pieces = [jnp.where(group == g, upper, 0.0) for g in range(GROUPS)]
         pieces += [jnp.where(later == g, lower, 0.0) for g in range(0, GROUPS, 2)]
         spread = jnp.concatenate(pieces, axis=0).astype(BF16)
-        found = dot_nt(spread, onehot[k])
+        found = dot(spread, turned_hot[k])
         first_part = found[0:144].reshape(9, 16, SPAN)
         second_part = found[144:216].reshape(9, 8, SPAN)
         if k == 0:
@@ -517,14 +573,16 @@
             scratch_shapes=held
             + [
                 pltpu.SemaphoreType.DMA((13,)),
-                pltpu.VMEM((8, 2 * BA), F32),
-                pltpu.VMEM((len(REACH), 8, 2 * BA), F32),
+                pltpu.VMEM((8, BA), F32),
+                pltpu.VMEM((len(REACH), 8, BA), F32),
                 pltpu.VMEM((144, SPAN), F32),
                 pltpu.VMEM((144, SPAN), BF16),
                 pltpu.VMEM((ATOMS // BA, 8 * K, BA), F32),
                 pltpu.VMEM((K, SPAN, ATOMS), BF16),
-                pltpu.VMEM((9, K, ATOMS), F32),
+                pltpu.VMEM((K, ATOMS, SPAN), BF16),
+                pltpu.VMEM((8, K, 8, ATOMS), F32),
                 pltpu.VMEM((8, K, ATOMS), F32),
+                pltpu.VMEM((K, 8, ATOMS), F32),
                 pltpu.VMEM((128, LAT), F32),
                 pltpu.VMEM((LAT, 16), BF16),
                 pltpu.VMEM((16, LAT), BF16),
@@ -546,6 +604,11 @@
                 pltpu.VMEM((K, 3 * C, ATOMS), F32),
                 pltpu.VMEM((K, C, ATOMS), F32),
                 pltpu.VMEM((ATOMS // BA, 8 * K, BA), F32),
+                pltpu.VMEM((8, 4 * K, 8, BA), F32),
+                pltpu.VMEM((K, 8, ATOMS), F32),
+                pltpu.VMEM((K, 8, ATOMS), F32),
+                pltpu.VMEM((K, 8, ATOMS), F32),
+                pltpu.VMEM((K, 8, ATOMS), F32),
                 pltpu.VMEM((K, 80, ATOMS), BF16),
                 pltpu.VMEM((K, LAT, ATOMS), BF16),
                 pltpu.VMEM((ATOMS // BA, 128, BA), F32),

time: 44.5 us -> 44 us (0.989)
  Pallas kernels: 41.7 us -> 41.1 us
    pallas_call x1, Pallas kernels: 41 us -> 40.5 us  [on_device(): pl.pallas_call(functools.partial(kernel, n_row, n_col), out_shape=jax.Sha...]
where the time goes in v3:
time: 44 us; the launch traced here: 43.8 us
  Pallas kernels  41.1 us (93%)
  between operations  1.94 us (4%)
  local copies, waits for them, and re-layouts  0.74 us (2%)
    pallas_call x1, Pallas kernels, on_device(): pl.pallas_call(functools.partial(kernel, n_row, n_col), out_shape=jax.Sha...  40.5 us

profile of v3, /device:TPU:2, one launch (start us, length us, event | category | flops | bytes accessed | tf_op | source)
XLA Modules:
  0.0 43.8 jit_solution(13636808311487342036)
XLA Ops:
  1.9 40.5 %shard_map.148.result = f32[13,1,512]{2,1,0:T(1,128)} custom-call(f32[1,3,1,256]{3,2,1,0:T(1,128)} %bitcast.9, s32[1,1,256]{2,1,0:T(1,128)} %spc.1, s32[1,1,256]{2,1,0:T(1,128)} %valid.1, s32[1,1]{1,0:T(1,128)S(6)} %copy.18.rcount, s32[1,1]{1,0:T(1,128)S(6)} %copy.19.ccount, s32[1,1,8,512]{3,2,1,0:T(8,128)} %nbr.1, f32[8]{0:T(128)} %rate.1, ...), custom_call_target="tpu_custom_call" | custom-call | tf_op jit(solution)/shard_map/pallas_call | solution.py:568
  42.4 0.0 copy-start
  42.4 0.7 %copy-done = f32[13,1,512]{2,1,0:T(1,128)S(1)} copy-done((f32[13,1,512]{2,1,0:T(1,128)S(1)}, f32[13,1,512]{2,1,0:T(1,128)}, u32[]{:S(2)}) %copy-start) | copy-done | bytes 26648
  43.2 0.6 %shard_map.149 = (f32[3,1,512]{2,1,0:T(1,128)}, f32[9,1,512]{2,1,0:T(1,128)}, f32[1,1,512]{2,1,0:T(1,128)}) custom-call(f32[13,1,512]{2,1,0:T(1,128)S(1)} %copy-done), custom_call_target="tpu_custom_call" | custom-call | tf_op jit(solution)/shard_map/pallas_call | solution.py:626
Async XLA Ops:
  42.4 0.7 %copy-start = (f32[13,1,512]{2,1,0:T(1,128)S(1)}, f32[13,1,512]{2,1,0:T(1,128)}, u32[]{:S(2)}) copy-start(f32[13,1,512]{2,1,0:T(1,128)} %shard_map.148.result) | copy-start | bytes 79876

commit v4 on v3

--- a/solution.py
+++ b/solution.py
@@ -27,6 +27,7 @@
 REACH = NEAR + [(2, b) for b in (-1, 0, 1)] + [(a, 2) for a in (-1, 0, 1)]
 DEGREE = [0, 1, 1, 1, 2, 2, 2, 2, 2]
 HALF = 256
+PARTS = ((0, 2, 6, 8, 3, 5), (1, 7, 4))
 STRIP = 16
 ROWS = 64
 BITE = 32
@@ -495,39 +496,45 @@
             vals[j, 8 * v : 8 * v + 8, :] = term[:, j * BA : j * BA + BA]
     vals[:, 96:128, :] = jnp.zeros((ATOMS // BA, 32, BA), F32)
 
-    for k in range(K):
-        group = jnp.broadcast_to(lax.shift_right_logical(nbr_v[0, 0, k : k + 1, :], 8), (8, ATOMS))
-        term = jnp.concatenate(
-            [vals[j, pl.ds(k, 16, stride=8), :] for j in range(ATOMS // BA)], axis=1
-        )
-        upper = term[0:8]
-        lower = term[8:16] + pltpu.roll(term[8:16], 4, 0)
-        later = group - jnp.where(row8 < 4, 0, 1)
-        pieces = [jnp.where(group == g, upper, 0.0) for g in range(GROUPS)]
-        pieces += [jnp.where(later == g, lower, 0.0) for g in range(0, GROUPS, 2)]
-        spread = jnp.concatenate(pieces, axis=0).astype(BF16)
-        found = dot(spread, turned_hot[k])
-        first_part = found[0:144].reshape(9, 16, SPAN)
-        second_part = found[144:216].reshape(9, 8, SPAN)
-        if k == 0:
-            ghost[:, 0:16, :] = first_part
-            ghost[:, 16:24, :] = second_part
-        else:
-            ghost[:, 0:16, :] += first_part
-            ghost[:, 16:24, :] += second_part
-
-    outs = []
-    for slot, (dr, dc) in enumerate(NEAR):
-        copy = pltpu.make_async_remote_copy(
-            src_ref=ghost.at[(dr + 1) * 3 + dc + 1],
-            dst_ref=ghost_in.at[slot],
-            send_sem=send_out.at[slot],
-            recv_sem=recv_out.at[slot],
-            device_id=at(dr, dc),
-            device_id_type=MESH,
-        )
-        copy.start()
-        outs.append(copy)
+    def scatter(blocks):
+        for k in range(K):
+            group = jnp.broadcast_to(lax.shift_right_logical(nbr_v[0, 0, k : k + 1, :], 8), (8, ATOMS))
+            term = jnp.concatenate(
+                [vals[j, pl.ds(k, 16, stride=8), :] for j in range(ATOMS // BA)], axis=1
+            )
+            upper = term[0:8]
+            lower = term[8:16] + pltpu.roll(term[8:16], 4, 0)
+            later = group - jnp.where(row8 < 4, 0, 1)
+            pieces = []
+            for b in blocks:
+                pieces += [jnp.where(group == 2 * b, upper, 0.0), jnp.where(group == 2 * b + 1, upper, 0.0)]
+                pieces += [jnp.where(later == 2 * b, lower, 0.0)]
+            found = dot(jnp.concatenate(pieces, axis=0).astype(BF16), turned_hot[k])
+            for i, b in enumerate(blocks):
+                part = found[24 * i : 24 * i + 24]
+                ghost[b] = part if k == 0 else ghost[b] + part
+
+    def send(blocks):
+        for b in blocks:
+            dr, dc = b // 3 - 1, b % 3 - 1
+            if (dr, dc) == (0, 0):
+                continue
+            slot = NEAR.index((dr, dc))
+            copy = pltpu.make_async_remote_copy(
+                src_ref=ghost.at[b],
+                dst_ref=ghost_in.at[slot],
+                send_sem=send_out.at[slot],
+                recv_sem=recv_out.at[slot],
+                device_id=at(dr, dc),
+                device_id_type=MESH,
+            )
+            copy.start()
+            outs[slot] = copy
+
+    outs = [None] * len(NEAR)
+    for blocks in PARTS:
+        scatter(blocks)
+        send(blocks)
     own_sums = jnp.concatenate([jnp.sum(t, axis=0, keepdims=True) for t in terms], axis=0)
     total = ghost[4]
     for slot, copy in enumerate(outs):

time: 44 us -> 43.4 us (0.986)
  Pallas kernels: 41.1 us -> 40.5 us
    pallas_call x1, Pallas kernels: 40.5 us -> 39.9 us  [on_device(): pl.pallas_call(functools.partial(kernel, n_row, n_col), out_shape=jax.Sha...]
where the time goes in v4:
time: 43.4 us; the launch traced here: 43.2 us
  Pallas kernels  40.5 us (93%)
  between operations  1.94 us (4%)
  local copies, waits for them, and re-layouts  0.74 us (2%)
    pallas_call x1, Pallas kernels, on_device(): pl.pallas_call(functools.partial(kernel, n_row, n_col), out_shape=jax.Sha...  39.9 us

profile of v4, /device:TPU:2, one launch (start us, length us, event | category | flops | bytes accessed | tf_op | source)
XLA Modules:
  0.0 43.2 jit_solution(18330521294860590269)
XLA Ops:
  1.9 39.9 %shard_map.148.result = f32[13,1,512]{2,1,0:T(1,128)} custom-call(f32[1,3,1,256]{3,2,1,0:T(1,128)} %bitcast.9, s32[1,1,256]{2,1,0:T(1,128)} %spc.1, s32[1,1,256]{2,1,0:T(1,128)} %valid.1, s32[1,1]{1,0:T(1,128)S(6)} %copy.18.rcount, s32[1,1]{1,0:T(1,128)S(6)} %copy.19.ccount, s32[1,1,8,512]{3,2,1,0:T(8,128)} %nbr.1, f32[8]{0:T(128)} %rate.1, ...), custom_call_target="tpu_custom_call" | custom-call | tf_op jit(solution)/shard_map/pallas_call | solution.py:575
  41.8 0.0 copy-start
  41.8 0.7 %copy-done = f32[13,1,512]{2,1,0:T(1,128)S(1)} copy-done((f32[13,1,512]{2,1,0:T(1,128)S(1)}, f32[13,1,512]{2,1,0:T(1,128)}, u32[]{:S(2)}) %copy-start) | copy-done | bytes 26648
  42.6 0.6 %shard_map.149 = (f32[3,1,512]{2,1,0:T(1,128)}, f32[9,1,512]{2,1,0:T(1,128)}, f32[1,1,512]{2,1,0:T(1,128)}) custom-call(f32[13,1,512]{2,1,0:T(1,128)S(1)} %copy-done), custom_call_target="tpu_custom_call" | custom-call | tf_op jit(solution)/shard_map/pallas_call | solution.py:633
Async XLA Ops:
  41.8 0.7 %copy-start = (f32[13,1,512]{2,1,0:T(1,128)S(1)}, f32[13,1,512]{2,1,0:T(1,128)}, u32[]{:S(2)}) copy-start(f32[13,1,512]{2,1,0:T(1,128)} %shard_map.148.result) | copy-start | bytes 79876
